TPU v7x, 32 devices: a whole 2x2x4 slice. The times are simulated.
32 devices in a mesh: az: 8 (over z, y), ax: 4 (over x, core).
Axes of the slice: x: 2, y: 2, z: 4, core: 2. Of those that a mesh axis runs over, the one named last changes fastest.
Arguments:
- start_field: float32 [16, 3, 16, 32, 512], P(None, None, 'az', 'ax'), may hold values from -4 to 4
- reluctivity: float32 [3, 16, 32, 512], P(None, 'az', 'ax'), may hold values from 0.05 to 1
- lamination: int32 [16, 32, 512], P('az', 'ax'), may hold values 0 or 1
- magnets: int32 [16, 32, 512], P('az', 'ax'), may hold values 0 or 1
- region_ids: int32 [16, 32, 512], P('az', 'ax'), may hold values from 0 to 31, as said below
- pieces: float32 [3, 16, 32], P(None, None, 'az'), may hold values from -5 to 5
- slot_map: int32 [16, 32], replicated, may hold values from 0 to 31, each once within a row
Outputs:
- solution_field: float32 [16, 3, 16, 32, 512], P(None, None, 'az', 'ax')
- residual: float32 [16, 3, 16, 32, 512], P(None, None, 'az', 'ax')
Inputs may be any that keep to these rules, and one draw needn't show every extreme that they name: `region_ids`: a cell of azimuthal sector s, the cells s * 2 to (s + 1) * 2 - 1 along the azimuth, holds a slot from s * 4 to (s + 1) * 4 - 1. `slot_map`: each row is a permutation.
All inputs are finite; a program needn't handle non-finite values. No bound on the sum of `lamination` or of `magnets` on one device may be relied on, other than what follows from the above.
Results may differ from a plain program's by a relative error of at most 0.00002.
Values sent between devices are 32-bit elements; how exact they have to be, the bound alone decides.
A program may use at most 128 MiB of HBM per device.

v0:
```python
import jax
import jax.numpy as jnp
from jax import lax
from jax.sharding import PartitionSpec as P

mass_term = 1.0
cheb_centre = 8.5
cheb_halfwidth = 7.5
cheb_sigma = cheb_centre / cheb_halfwidth
rho_first = 1.0 / cheb_sigma
rho_second = 1.0 / (2.0 * cheb_sigma - rho_first)


def passed_along(value, axis, steps):
    count = lax.axis_size(axis)
    pairs = [(source, (source + steps) % count) for source in range(count)]
    return lax.ppermute(value, axis, pairs)


def from_behind(value, axis, steps):
    count = lax.axis_size(axis)
    first, last = (max(0, -steps), min(count, count - steps))
    return lax.ppermute(value, axis, [(source, source + steps) for source in range(first, last)])


def radial_forward(values):
    return jnp.concatenate([values[..., 1:], jnp.zeros_like(values[..., :1])], axis=-1) - values


def radial_backward(values):
    return values - jnp.concatenate([jnp.zeros_like(values[..., :1]), values[..., :-1]], axis=-1)


def curl_forward(core, along_a1, along_a2, along_z0, along_z2):
    return jnp.stack(
        [
            along_z2 - radial_forward(core[:, 1]),
            radial_forward(core[:, 0]) - along_a2,
            along_a1 - along_z0,
        ],
        axis=1,
    )


def curl_backward(core, along_a1, along_a2, along_z0, along_z2):
    return jnp.stack(
        [
            along_z2 - radial_backward(core[:, 1]),
            radial_backward(core[:, 0]) - along_a2,
            along_a1 - along_z0,
        ],
        axis=1,
    )


def residual_shifts(field, reluct, source):
    ahead_az = passed_along(field[:, 1:3, 0:1], "az", -1)
    ahead_ax = from_behind(jnp.stack([field[:, 0, :, 0:1], field[:, 2, :, 0:1]], axis=1), "ax", -1)
    step_az = jnp.concatenate([field[:, 1:3, 1:], ahead_az], axis=2) - field[:, 1:3]
    pair_field = jnp.stack([field[:, 0], field[:, 2]], axis=1)
    step_ax = jnp.concatenate([pair_field[:, :, :, 1:], ahead_ax], axis=3) - pair_field
    flux = curl_forward(field, step_az[:, 0], step_az[:, 1], step_ax[:, 0], step_ax[:, 1])
    intensity = reluct[None] * (flux - source)
    behind_az = passed_along(intensity[:, 1:3, -1:], "az", 1)
    behind_ax = from_behind(
        jnp.stack([intensity[:, 0, :, -1:], intensity[:, 2, :, -1:]], axis=1), "ax", 1
    )
    back_step_az = intensity[:, 1:3] - jnp.concatenate([behind_az, intensity[:, 1:3, :-1]], axis=2)
    pair_inten = jnp.stack([intensity[:, 0], intensity[:, 2]], axis=1)
    back_step_ax = pair_inten - jnp.concatenate([behind_ax, pair_inten[:, :, :, :-1]], axis=3)
    curl = curl_backward(
        intensity, back_step_az[:, 0], back_step_az[:, 1], back_step_ax[:, 0], back_step_ax[:, 1]
    )
    return -curl - mass_term * field


def shards(start_field, reluctivity, lamination, magnets, region_ids, pieces, slot_map):
    devs, comps, cells_az, cells_ax, radial = start_field.shape
    axial = jnp.array([0.0, 1.0, 0.0], jnp.float32)
    reluct = reluctivity * (
        1.0 + 3.0 * lamination.astype(jnp.float32)[None] * axial[:, None, None, None]
    )
    every_piece = lax.all_gather(pieces, "az", axis=2, tiled=True)
    slots_here = pieces.shape[2]
    base = lax.axis_index("az") * slots_here
    local_map = lax.dynamic_slice_in_dim(slot_map, base, slots_here, 1)
    local_table = jnp.take_along_axis(
        every_piece, jnp.broadcast_to(local_map[None], (comps, devs, slots_here)), axis=2
    )
    offset = (region_ids - base)[None, None]
    source = jnp.zeros(start_field.shape, jnp.float32)
    for slot in range(slots_here):
        values = jnp.transpose(local_table[:, :, slot])[:, :, None, None, None]
        source = jnp.where(offset == slot, values, source)
    source = source * magnets.astype(jnp.float32)[None, None]

    def residual_fn(field):
        return residual_shifts(field, reluct, source)

    first_res = residual_fn(start_field)
    first_dir = first_res / cheb_centre
    middle = start_field + first_dir
    second_res = residual_fn(middle)
    second_dir = rho_second * rho_first * first_dir + 2.0 * rho_second / cheb_halfwidth * second_res
    final = middle + second_dir
    return (final, residual_fn(final))


def solution(mesh):
    placed = (
        P(None, None, "az", "ax", None),
        P(None, "az", "ax", None),
        P("az", "ax", None),
        P("az", "ax", None),
        P("az", "ax", None),
        P(None, None, "az"),
        P(),
    )
    return jax.shard_map(
        shards,
        mesh=mesh,
        in_specs=placed,
        out_specs=(P(None, None, "az", "ax", None), P(None, None, "az", "ax", None)),
        check_vma=False,
    )
```

profile of v0, /device:TPU:0, one launch (start us, length us, event | category | flops | bytes accessed | tf_op | source)
XLA Modules:
  0.0 154.9 jit_solution(8908655718597038340)
XLA Ops:
  0.6 1.4 fusion.57
  2.2 1.3 collective-permute-start
  3.5 2.3 %fusion.56 = (f32[16,2,1,8,512]{4,3,2,0,1:T(8,128)}, f32[16,2,1,8,512]{4,3,2,0,1:T(8,128)}) fusion(f32[16,3,2,8,512]{4,3,2,1,0:T(8,128)} %param.8), kind=kLoop, calls=%fused_computation.144 | loop fusion | bytes 2097152 | tf_op jit(solution)/shard_map/slice | solution.py:59
  5.7 6.0 %collective-permute-start.1 = (f32[16,2,1,8,512]{4,3,2,0,1:T(8,128)}, f32[16,2,1,8,512]{4,3,2,0,1:T(8,128)}, u32[]{:S(2)}, u32[]{:S(2)}) collective-permute-start(f32[16,2,1,8,512]{4,3,2,0,1:T(8,128)} %get-tuple-element.77), channel_id=1, source_target_pairs={{0,28},{4,0},{8,4},{12,8},{16,12},{20,16},{24,20},{28,24},{1,29},{... | collective-permute-start | bytes 1572872 | tf_op jit(solution)/shard_map/ppermute | solution.py:17
  11.7 1.1 slice_bitcast_fusion.17
  12.8 35.3 %all_gather.3 = f32[3,16,32]{1,0,2:T(4,128)S(1)} all-gather(f32[3,16,4]{1,0,2:T(4,128)S(1)} %copy.91), channel_id=1, replica_groups=mesh['az'=8,'ax'=4] {'az'}, dimensions={2}, use_global_device_ids=true | all-gather | bytes 6912 | tf_op jit(solution)/shard_map/all_gather | solution.py:83
  48.3 2.1 %gather_fusion = f32[192]{0:T(256)S(1)} fusion(f32[3,16,32]{1,0,2:T(4,128)S(1)} %all_gather.3, s32[192]{0:T(256)S(1)} %reshape.31), kind=kCustom, calls=%fused_computation | custom fusion | bytes 3840 | tf_op jit(solution)/shard_map/jit(take_along_axis)/gather | solution.py:87
  51.6 1.2 slice.393
  54.4 1.3 slice_subtract_fusion.5
  56.1 1.0 fusion
  57.4 1.3 collective-permute-start.2
  58.7 2.3 %collective-permute-start.3 = (f32[16,2,1,8,512]{4,3,2,0,1:T(8,128)S(1)}, f32[16,2,1,8,512]{4,3,2,0,1:T(8,128)S(1)}, u32[]{:S(2)}, u32[]{:S(2)}) collective-permute-start(f32[16,2,1,8,512]{4,3,2,0,1:T(8,128)S(1)} %get-tuple-element.66), channel_id=1, source_target_pairs={{0,4},{4,8},{8,12},{12,16},{16,20},{20,24},{24,28},{28,0},{1,5},{5... | collective-permute-start | bytes 1572872 | tf_op jit(solution)/shard_map/ppermute | solution.py:17
  61.7 12.8 %collective-permute-done.3 = f32[16,2,1,8,512]{4,3,2,0,1:T(8,128)S(1)} collective-permute-done((f32[16,2,1,8,512]{4,3,2,0,1:T(8,128)S(1)}, f32[16,2,1,8,512]{4,3,2,0,1:T(8,128)S(1)}, u32[]{:S(2)}, u32[]{:S(2)}) %collective-permute-start.3) | collective-permute-done | bytes 524320 | tf_op jit(solution)/shard_map/ppermute | solution.py:17
  75.9 1.3 collective-permute-start.4
  77.2 2.4 %collective-permute-start.5 = (f32[16,2,1,8,512]{4,3,2,0,1:T(8,128)S(1)}, f32[16,2,1,8,512]{4,3,2,0,1:T(8,128)S(1)}, u32[]{:S(2)}, u32[]{:S(2)}) collective-permute-start(f32[16,2,1,8,512]{4,3,2,0,1:T(8,128)S(1)} %get-tuple-element.57), channel_id=1, source_target_pairs={{0,28},{4,0},{8,4},{12,8},{16,12},{20,16},{24,20},{28,24},{1,29},{... | collective-permute-start | bytes 1572872 | tf_op jit(solution)/shard_map/ppermute | solution.py:17
  80.8 9.8 %collective-permute-done.5 = f32[16,2,1,8,512]{4,3,2,0,1:T(8,128)S(1)} collective-permute-done((f32[16,2,1,8,512]{4,3,2,0,1:T(8,128)S(1)}, f32[16,2,1,8,512]{4,3,2,0,1:T(8,128)S(1)}, u32[]{:S(2)}, u32[]{:S(2)}) %collective-permute-start.5) | collective-permute-done | bytes 524320 | tf_op jit(solution)/shard_map/ppermute | solution.py:17
  92.6 3.3 %collective-permute-start.6 = (f32[16,2,2,1,512]{4,3,2,0,1:T(1,128)S(1)}, f32[16,2,2,1,512]{4,3,2,0,1:T(1,128)S(1)}, u32[]{:S(2)}, u32[]{:S(2)}) collective-permute-start(f32[16,2,2,1,512]{4,3,2,0,1:T(1,128)S(1)} %pad_maximum_fusion.10), channel_id=1, source_target_pairs={{0,1},{1,2},{2,3},{4,5},{5,6},{6,7},{8,9},{9,10},{10,11},{12,13},{... | collective-permute-start | bytes 393224 | tf_op jit(solution)/shard_map/ppermute | solution.py:23
  97.2 15.7 %collective-permute-done.7 = f32[16,2,1,8,512]{4,3,2,0,1:T(8,128)S(1)} collective-permute-done((f32[16,2,1,8,512]{4,3,2,0,1:T(8,128)S(1)}, f32[16,2,1,8,512]{4,3,2,0,1:T(8,128)S(1)}, u32[]{:S(2)}, u32[]{:S(2)}) %collective-permute-start.7) | collective-permute-done | bytes 524320 | tf_op jit(solution)/shard_map/ppermute | solution.py:17
  114.6 1.3 collective-permute-start.8
  115.9 2.0 %collective-permute-start.9 = (f32[16,2,1,8,512]{4,3,2,0,1:T(8,128)S(1)}, f32[16,2,1,8,512]{4,3,2,0,1:T(8,128)S(1)}, u32[]{:S(2)}, u32[]{:S(2)}) collective-permute-start(f32[16,2,1,8,512]{4,3,2,0,1:T(8,128)S(1)} %get-tuple-element.37), channel_id=1, source_target_pairs={{0,28},{4,0},{8,4},{12,8},{16,12},{20,16},{24,20},{28,24},{1,29},{... | collective-permute-start | bytes 1572872 | tf_op jit(solution)/shard_map/ppermute | solution.py:17
  119.0 11.7 %collective-permute-done.9 = f32[16,2,1,8,512]{4,3,2,0,1:T(8,128)S(1)} collective-permute-done((f32[16,2,1,8,512]{4,3,2,0,1:T(8,128)S(1)}, f32[16,2,1,8,512]{4,3,2,0,1:T(8,128)S(1)}, u32[]{:S(2)}, u32[]{:S(2)}) %collective-permute-start.9) | collective-permute-done | bytes 524320 | tf_op jit(solution)/shard_map/ppermute | solution.py:17
  132.8 2.0 %collective-permute-start.10 = (f32[16,2,2,1,512]{4,3,2,0,1:T(1,128)S(1)}, f32[16,2,2,1,512]{4,3,2,0,1:T(1,128)S(1)}, u32[]{:S(2)}, u32[]{:S(2)}) collective-permute-start(f32[16,2,2,1,512]{4,3,2,0,1:T(1,128)S(1)} %pad_maximum_fusion.12), channel_id=1, source_target_pairs={{0,1},{1,2},{2,3},{4,5},{5,6},{6,7},{8,9},{9,10},{10,11},{12,13},{... | collective-permute-start | bytes 393224 | tf_op jit(solution)/shard_map/ppermute | solution.py:23
  136.1 15.3 %collective-permute-done.11 = f32[16,2,1,8,512]{4,3,2,0,1:T(8,128)S(1)} collective-permute-done((f32[16,2,1,8,512]{4,3,2,0,1:T(8,128)S(1)}, f32[16,2,1,8,512]{4,3,2,0,1:T(8,128)S(1)}, u32[]{:S(2)}, u32[]{:S(2)}) %collective-permute-start.11) | collective-permute-done | bytes 524320 | tf_op jit(solution)/shard_map/ppermute | solution.py:17
  152.1 2.8 %fusion.8 = (f32[16,3,2,8,512]{4,3,2,1,0:T(8,128)}, f32[16,3,2,8,512]{4,3,2,1,0:T(8,128)}) fusion(f32[16,1,2,8,512]{4,3,2,1,0:T(8,128)S(1)} %slice_subtract_fusion.6, f32[16,1,2,8,512]{4,3,2,1,0:T(8,128)S(1)} %get-tuple-element.21, f32[16,1,2,8,512]{4,3,2,1,0:T(8,128)S(1)} %get-tuple-element.20, f32[16,1,2,8,512]{4,3,2,0,1:T(8,128)S(1)} %slice_subtract_fusion.8, ...), kind=kLoop, calls=%fused_computation.15 | loop fusion | flops 7077888 | bytes 9437184 | tf_op jit(solution)/shard_map/sub | solution.py:74
  (96 shorter events, 16.8 us)
Async XLA Ops:
  0.6 11.1 %copy-start = (f32[16,3,2,8,512]{4,3,2,1,0:T(8,128)S(1)}, f32[16,3,2,8,512]{4,3,2,1,0:T(8,128)}, u32[]{:S(2)}) copy-start(f32[16,3,2,8,512]{4,3,2,1,0:T(8,128)} %param.8) | copy-start | bytes 4718596
  2.2 51.2 %collective-permute-start = (f32[16,2,2,1,512]{4,3,2,0,1:T(1,128)S(1)}, f32[16,2,2,1,512]{4,3,2,0,1:T(1,128)S(1)}, u32[]{:S(2)}, u32[]{:S(2)}) collective-permute-start(f32[16,2,2,1,512]{4,3,2,0,1:T(1,128)S(1)} %pad_maximum_fusion.7), channel_id=1, source_target_pairs={{1,0},{2,1},{3,2},{5,4},{6,5},{7,6},{9,8},{10,9},{11,10},{13,12},{... | collective-permute-start | bytes 393224 | tf_op jit(solution)/shard_map/ppermute | solution.py:23
  5.7 7.1 %copy-start.6 = (f32[3,16,4]{1,2,0:T(4,128)S(1)}, f32[3,16,4]{1,2,0:T(4,128)}, u32[]{:S(2)}) copy-start(f32[3,16,4]{1,2,0:T(4,128)} %param.13) | copy-start | bytes 2308
  5.7 42.4 %copy-start.5 = (s32[16,32]{1,0:T(8,128)S(1)}, s32[16,32]{1,0:T(8,128)}, u32[]{:S(2)}) copy-start(s32[16,32]{1,0:T(8,128)} %param.14) | copy-start | bytes 6148
  5.7 47.9 %collective-permute-start.1 = (f32[16,2,1,8,512]{4,3,2,0,1:T(8,128)}, f32[16,2,1,8,512]{4,3,2,0,1:T(8,128)}, u32[]{:S(2)}, u32[]{:S(2)}) collective-permute-start(f32[16,2,1,8,512]{4,3,2,0,1:T(8,128)} %get-tuple-element.77), channel_id=1, source_target_pairs={{0,28},{4,0},{8,4},{12,8},{16,12},{20,16},{24,20},{28,24},{1,29},{... | collective-permute-start | bytes 1572872 | tf_op jit(solution)/shard_map/ppermute | solution.py:17
  48.3 2.3 %copy-start.3 = (s32[2,8,512]{2,1,0:T(8,128)S(1)}, s32[2,8,512]{2,1,0:T(8,128)}, u32[]{:S(2)}) copy-start(s32[2,8,512]{2,1,0:T(8,128)} %param.10) | copy-start | bytes 98308
  50.5 2.6 %copy-start.7 = (f32[3]{0:T(128)S(1)}, f32[3]{0:T(128)}, u32[]{:S(2)}) copy-start(f32[3]{0:T(128)} %constant.50.clone) | copy-start | bytes 40
  50.6 2.5 %copy-start.4 = (s32[2,8,512]{2,1,0:T(8,128)S(1)}, s32[2,8,512]{2,1,0:T(8,128)}, u32[]{:S(2)}) copy-start(s32[2,8,512]{2,1,0:T(8,128)} %param.11) | copy-start | bytes 98308
  50.6 2.5 %copy-start.2 = (f32[3,2,8,512]{3,2,1,0:T(8,128)S(1)}, f32[3,2,8,512]{3,2,1,0:T(8,128)}, u32[]{:S(2)}) copy-start(f32[3,2,8,512]{3,2,1,0:T(8,128)} %param.9) | copy-start | bytes 294916
  53.3 1.0 copy-start.1
  57.4 3.9 %collective-permute-start.2 = (f32[16,2,2,1,512]{4,3,2,0,1:T(1,128)S(1)}, f32[16,2,2,1,512]{4,3,2,0,1:T(1,128)S(1)}, u32[]{:S(2)}, u32[]{:S(2)}) collective-permute-start(f32[16,2,2,1,512]{4,3,2,0,1:T(1,128)S(1)} %pad_maximum_fusion.8), channel_id=1, source_target_pairs={{0,1},{1,2},{2,3},{4,5},{5,6},{6,7},{8,9},{9,10},{10,11},{12,13},{... | collective-permute-start | bytes 393224 | tf_op jit(solution)/shard_map/ppermute | solution.py:23
  58.7 15.8 %collective-permute-start.3 = (f32[16,2,1,8,512]{4,3,2,0,1:T(8,128)S(1)}, f32[16,2,1,8,512]{4,3,2,0,1:T(8,128)S(1)}, u32[]{:S(2)}, u32[]{:S(2)}) collective-permute-start(f32[16,2,1,8,512]{4,3,2,0,1:T(8,128)S(1)} %get-tuple-element.66), channel_id=1, source_target_pairs={{0,4},{4,8},{8,12},{12,16},{16,20},{20,24},{24,28},{28,0},{1,5},{5... | collective-permute-start | bytes 1572872 | tf_op jit(solution)/shard_map/ppermute | solution.py:17
  75.9 4.6 %collective-permute-start.4 = (f32[16,2,2,1,512]{4,3,2,0,1:T(1,128)S(1)}, f32[16,2,2,1,512]{4,3,2,0,1:T(1,128)S(1)}, u32[]{:S(2)}, u32[]{:S(2)}) collective-permute-start(f32[16,2,2,1,512]{4,3,2,0,1:T(1,128)S(1)} %pad_maximum_fusion.9), channel_id=1, source_target_pairs={{1,0},{2,1},{3,2},{5,4},{6,5},{7,6},{9,8},{10,9},{11,10},{13,12},{... | collective-permute-start | bytes 393224 | tf_op jit(solution)/shard_map/ppermute | solution.py:23
  77.2 13.4 %collective-permute-start.5 = (f32[16,2,1,8,512]{4,3,2,0,1:T(8,128)S(1)}, f32[16,2,1,8,512]{4,3,2,0,1:T(8,128)S(1)}, u32[]{:S(2)}, u32[]{:S(2)}) collective-permute-start(f32[16,2,1,8,512]{4,3,2,0,1:T(8,128)S(1)} %get-tuple-element.57), channel_id=1, source_target_pairs={{0,28},{4,0},{8,4},{12,8},{16,12},{20,16},{24,20},{28,24},{1,29},{... | collective-permute-start | bytes 1572872 | tf_op jit(solution)/shard_map/ppermute | solution.py:17
  92.6 4.2 %collective-permute-start.6 = (f32[16,2,2,1,512]{4,3,2,0,1:T(1,128)S(1)}, f32[16,2,2,1,512]{4,3,2,0,1:T(1,128)S(1)}, u32[]{:S(2)}, u32[]{:S(2)}) collective-permute-start(f32[16,2,2,1,512]{4,3,2,0,1:T(1,128)S(1)} %pad_maximum_fusion.10), channel_id=1, source_target_pairs={{0,1},{1,2},{2,3},{4,5},{5,6},{6,7},{8,9},{9,10},{10,11},{12,13},{... | collective-permute-start | bytes 393224 | tf_op jit(solution)/shard_map/ppermute | solution.py:23
  95.9 17.0 %collective-permute-start.7 = (f32[16,2,1,8,512]{4,3,2,0,1:T(8,128)S(1)}, f32[16,2,1,8,512]{4,3,2,0,1:T(8,128)S(1)}, u32[]{:S(2)}, u32[]{:S(2)}) collective-permute-start(f32[16,2,1,8,512]{4,3,2,0,1:T(8,128)S(1)} %get-tuple-element.46), channel_id=1, source_target_pairs={{0,4},{4,8},{8,12},{12,16},{16,20},{20,24},{24,28},{28,0},{1,5},{5... | collective-permute-start | bytes 1572872 | tf_op jit(solution)/shard_map/ppermute | solution.py:17
  114.6 4.1 %collective-permute-start.8 = (f32[16,2,2,1,512]{4,3,2,0,1:T(1,128)S(1)}, f32[16,2,2,1,512]{4,3,2,0,1:T(1,128)S(1)}, u32[]{:S(2)}, u32[]{:S(2)}) collective-permute-start(f32[16,2,2,1,512]{4,3,2,0,1:T(1,128)S(1)} %pad_maximum_fusion.11), channel_id=1, source_target_pairs={{1,0},{2,1},{3,2},{5,4},{6,5},{7,6},{9,8},{10,9},{11,10},{13,12},{... | collective-permute-start | bytes 393224 | tf_op jit(solution)/shard_map/ppermute | solution.py:23
  115.9 14.9 %collective-permute-start.9 = (f32[16,2,1,8,512]{4,3,2,0,1:T(8,128)S(1)}, f32[16,2,1,8,512]{4,3,2,0,1:T(8,128)S(1)}, u32[]{:S(2)}, u32[]{:S(2)}) collective-permute-start(f32[16,2,1,8,512]{4,3,2,0,1:T(8,128)S(1)} %get-tuple-element.37), channel_id=1, source_target_pairs={{0,28},{4,0},{8,4},{12,8},{16,12},{20,16},{24,20},{28,24},{1,29},{... | collective-permute-start | bytes 1572872 | tf_op jit(solution)/shard_map/ppermute | solution.py:17
  132.8 3.0 %collective-permute-start.10 = (f32[16,2,2,1,512]{4,3,2,0,1:T(1,128)S(1)}, f32[16,2,2,1,512]{4,3,2,0,1:T(1,128)S(1)}, u32[]{:S(2)}, u32[]{:S(2)}) collective-permute-start(f32[16,2,2,1,512]{4,3,2,0,1:T(1,128)S(1)} %pad_maximum_fusion.12), channel_id=1, source_target_pairs={{0,1},{1,2},{2,3},{4,5},{5,6},{6,7},{8,9},{9,10},{10,11},{12,13},{... | collective-permute-start | bytes 393224 | tf_op jit(solution)/shard_map/ppermute | solution.py:23
  134.8 16.6 %collective-permute-start.11 = (f32[16,2,1,8,512]{4,3,2,0,1:T(8,128)S(1)}, f32[16,2,1,8,512]{4,3,2,0,1:T(8,128)S(1)}, u32[]{:S(2)}, u32[]{:S(2)}) collective-permute-start(f32[16,2,1,8,512]{4,3,2,0,1:T(8,128)S(1)} %get-tuple-element.26), channel_id=1, source_target_pairs={{0,4},{4,8},{8,12},{12,16},{16,20},{20,24},{24,28},{28,0},{1,5},{5... | collective-permute-start | bytes 1572872 | tf_op jit(solution)/shard_map/ppermute | solution.py:17
where the time goes:
time: 155 us
  waiting for transfers between devices  66.1 us (43%)
  blocking collectives  35.3 us (23%)
  starting transfers between devices  23.6 us (15%)
  other arithmetic  16.3 us (11%)
  local copies, waits for them, and re-layouts  12.4 us (8%)
    ppermute x6, waiting for transfers between devices, passed_along(): return lax.ppermute(value, axis, pairs)  65.3 us
    all_gather x1, blocking collectives, shards(): every_piece = lax.all_gather(pieces, 'az', axis=2, tiled=True)  35.3 us
    ppermute x6, starting transfers between devices, passed_along(): return lax.ppermute(value, axis, pairs)  13.2 us
    ppermute x6, starting transfers between devices, from_behind(): lax.ppermute(value, axis, [(source, source + steps) for source in range(f...  10.5 us
  transfers between devices with their start and end apart: 12, of which 8 were waited for; matrix products, arithmetic and copies ran while one was open for 8% of the time, Pallas kernels for 0%

commit v1 on v0

v1 whole, which is shorter than its diff:
```python
import functools

import jax
import jax.numpy as jnp
from jax import lax
from jax.experimental import pallas as pl
from jax.experimental.pallas import tpu as pltpu
from jax.sharding import PartitionSpec as P

mass_term = 1.0
cheb_centre = 8.5
cheb_halfwidth = 7.5
cheb_sigma = cheb_centre / cheb_halfwidth
rho_first = 1.0 / cheb_sigma
rho_second = 1.0 / (2.0 * cheb_sigma - rho_first)

MESH = pl.DeviceIdType.MESH
F32 = jnp.float32
LEVELS = 3


def kernel(
    n_az, n_ax, devs, cells, slots,
    start, rel, lam, mag, reg, pcs, smap,
    sol, res,
    X, D0, I, NS, RS, G, PG, TAB, ZA, ZI, AA, AI, SA, SI,
    in_loc, in_s, in_r, g_s, g_r, p_s, p_r,
    za_s, za_r, zi_s, zi_r, aa_s, aa_r, ai_s, ai_r, o_s, o_r, o_l,
):
    half = devs // 2
    planes = 2 * cells
    rows, radial = X.shape[-2], X.shape[-1]
    az, ax = lax.axis_index("az"), lax.axis_index("ax")
    side = lax.rem(az, 2)
    partner = az + 1 - 2 * side
    up, down = lax.rem(az + 2, n_az), lax.rem(az + n_az - 2, n_az)
    mine = pl.ds(cells * side, cells)
    theirs = pl.ds(cells * (1 - side), cells)
    has_below, has_above = ax > 0, ax < n_ax - 1

    def remote(src, dst, s, r, where):
        return pltpu.make_async_remote_copy(
            src_ref=src, dst_ref=dst, send_sem=s, recv_sem=r, device_id=where, device_id_type=MESH
        )

    def local_in():
        return pltpu.make_async_copy(start.at[pl.ds(half * side, half)], X.at[0, :, :, mine], in_loc)

    def swap_in(k):
        return remote(
            start.at[half * (1 - side) + k], X.at[0, k, :, mine], in_s.at[k], in_r.at[k], {"az": partner}
        )

    def swap_g():
        return remote(G.at[:, mine], G.at[:, mine], g_s, g_r, {"az": partner})

    def give_pieces(step):
        return remote(PG.at[az], PG.at[az], p_s.at[step], p_r.at[step], {"az": lax.rem(az + step, n_az)})

    def z_a(level, k):
        return remote(
            X.at[level, k, 1:3, 0], ZA.at[level, k], za_s.at[level, k], za_r.at[level, k], {"az": down}
        )

    def z_i(level, k):
        return remote(
            I.at[level, k, 1:3, planes - 1], ZI.at[level, k], zi_s.at[level, k], zi_r.at[level, k], {"az": up}
        )

    def ax_a(level, k):
        return remote(SA.at[level, k], AA.at[level, k], aa_s.at[level, k], aa_r.at[level, k], {"ax": ax - 1})

    def ax_i(level, k):
        return remote(SI.at[level, k], AI.at[level, k], ai_s.at[level, k], ai_r.at[level, k], {"ax": ax + 1})

    def out_away(which, k):
        src, dst = ((X.at[2, k], sol), (RS.at[k], res))[which]
        return remote(
            src.at[:, theirs], dst.at[half * side + k], o_s.at[which, k], o_r.at[which, k], {"az": partner}
        )

    def out_here(which, k):
        src, dst = ((X.at[2, k], sol), (RS.at[k], res))[which]
        return pltpu.make_async_copy(src.at[:, mine], dst.at[half * side + k], o_l.at[which, k])

    local_in().start()
    barrier = pltpu.get_barrier_semaphore()
    for step in range(1, n_az):
        pl.semaphore_signal(
            barrier, inc=1, device_id={"az": lax.rem(az + step, n_az)}, device_id_type=MESH
        )

    @pl.when(has_below)
    def _():
        pl.semaphore_signal(barrier, inc=1, device_id={"ax": ax - 1}, device_id_type=MESH)

    @pl.when(has_above)
    def _():
        pl.semaphore_signal(barrier, inc=1, device_id={"ax": ax + 1}, device_id_type=MESH)

    for p in range(cells):
        G[0, cells * side + p] = rel[0, p]
        G[1, cells * side + p] = rel[1, p] * (1.0 + 3.0 * lam[p].astype(F32))
        G[2, cells * side + p] = rel[2, p]
        G[3, cells * side + p] = jnp.where(mag[p] == 1, reg[p] - az * slots, -1).astype(F32)
    PG[az] = pcs[...]

    pl.semaphore_wait(barrier, n_az - 1 + has_below.astype(jnp.int32) + has_above.astype(jnp.int32))

    swap_in(0).start()
    for step in range(1, n_az):
        give_pieces(step).start()
    swap_g().start()

    def start_in(k, carry):
        swap_in(k).start()
        return carry

    lax.fori_loop(1, half, start_in, 0)

    @pl.when(jnp.logical_not(has_above))
    def _():
        AA[...] = jnp.zeros_like(AA)

    @pl.when(jnp.logical_not(has_below))
    def _():
        AI[...] = jnp.zeros_like(AI)

    row_of = lax.broadcasted_iota(jnp.int32, (rows, radial), 0)
    lane_of = lax.broadcasted_iota(jnp.int32, (rows, radial), 1)

    def next_radial(v):
        return jnp.where(lane_of == radial - 1, 0.0, pltpu.roll(v, radial - 1, 1))

    def prev_radial(v):
        return jnp.where(lane_of == 0, 0.0, pltpu.roll(v, 1, 1))

    def next_axial(v, halo):
        return jnp.where(row_of == rows - 1, halo, pltpu.roll(v, rows - 1, 0))

    def prev_axial(v, halo):
        return jnp.where(row_of == 0, halo, pltpu.roll(v, 1, 0))

    def send_a(level, k):
        z_a(level, k).start()
        for p in range(planes):
            for j, c in enumerate((0, 2)):
                SA[level, k, j * planes + p : j * planes + p + 1, :] = X[level, k, c, p, 0:1, :]

        @pl.when(has_below)
        def _():
            ax_a(level, k).start()

    def sources(k):
        table = TAB[...]
        lane = lax.broadcasted_iota(jnp.int32, table.shape, 1)
        for c in range(3):
            column = jnp.sum(
                jnp.where(lane == c * devs + half * side + k, table, 0.0), axis=1, keepdims=True
            )
            values = [jnp.broadcast_to(column[j : j + 1], (rows, radial)) for j in range(2 * slots)]
            for p in range(planes):
                code = G[3, p]
                total = jnp.zeros((rows, radial), F32)
                for j in range(slots):
                    total = jnp.where(code == float(j), values[p // cells * slots + j], total)
                NS[k, c, p] = G[c, p] * total

    def intensity(level, k):
        z_a(level, k).wait_recv()

        @pl.when(has_above)
        def _():
            ax_a(level, k).wait_recv()

        for p in reversed(range(planes)):
            a0, a1, a2 = X[level, k, 0, p], X[level, k, 1, p], X[level, k, 2, p]
            if p < planes - 1:
                b1, b2 = X[level, k, 1, p + 1], X[level, k, 2, p + 1]
            else:
                b1, b2 = ZA[level, k, 0], ZA[level, k, 1]
            h0 = AA[level, k, p : p + 1, :]
            h2 = AA[level, k, planes + p : planes + p + 1, :]
            f0 = (next_axial(a2, h2) - a2) - (next_radial(a1) - a1)
            f1 = (next_radial(a0) - a0) - (b2 - a2)
            f2 = (b1 - a1) - (next_axial(a0, h0) - a0)
            for c, f in enumerate((f0, f1, f2)):
                value = G[c, p] * f - NS[k, c, p]
                I[level, k, c, p] = value
                if c != 1:
                    at = (0 if c == 0 else planes) + p
                    SI[level, k, at : at + 1, :] = value[rows - 1 : rows, :]
            if p == planes - 1:
                z_i(level, k).start()

        @pl.when(has_above)
        def _():
            ax_i(level, k).start()

    def curl(level, k):
        z_i(level, k).wait_recv()

        @pl.when(has_below)
        def _():
            ax_i(level, k).wait_recv()

        for p in range(planes):
            i0, i1, i2 = I[level, k, 0, p], I[level, k, 1, p], I[level, k, 2, p]
            if p > 0:
                b1, b2 = I[level, k, 1, p - 1], I[level, k, 2, p - 1]
            else:
                b1, b2 = ZI[level, k, 0], ZI[level, k, 1]
            h0 = AI[level, k, p : p + 1, :]
            h2 = AI[level, k, planes + p : planes + p + 1, :]
            c0 = (i2 - prev_axial(i2, h2)) - (i1 - prev_radial(i1))
            c1 = (i0 - prev_radial(i0)) - (i2 - b2)
            c2 = (i1 - b1) - (i0 - prev_axial(i0, h0))
            for c, value in enumerate((c0, c1, c2)):
                field = X[level, k, c, p]
                r = -value - mass_term * field
                if level == 0:
                    d = r * (1.0 / cheb_centre)
                    D0[k, c, p] = d
                    X[1, k, c, p] = field + d
                elif level == 1:
                    d = (rho_second * rho_first) * D0[k, c, p] + (2.0 * rho_second / cheb_halfwidth) * r
                    X[2, k, c, p] = field + d
                else:
                    RS[k, c, p] = r
        if level < 2:
            send_a(level + 1, k)
        if level > 0:
            out_away(level - 1, k).start()
            out_here(level - 1, k).start()

    def stage(s, k):
        if s == 0:
            @pl.when(k == 0)
            def _():
                local_in().wait()

            swap_in(k).wait_recv()
            send_a(0, k)
        elif s == 1:
            @pl.when(k == 0)
            def _():
                for step in range(1, n_az):
                    give_pieces(step).wait_recv()
                own = smap[...]

                def add(p, total):
                    for q in range(slots):
                        total = total + jnp.where(own == p * slots + q, PG[p, q : q + 1, :], 0.0)
                    return total

                TAB[...] = lax.fori_loop(0, n_az, add, jnp.zeros(TAB.shape, F32))
                swap_g().wait_recv()

            sources(k)
            intensity(0, k)
        elif s % 2 == 0:
            curl(s // 2 - 1, k)
        else:
            intensity(s // 2, k)

    stages = 1 + 2 * LEVELS

    def wave(t, carry):
        for s in reversed(range(stages)):
            k = t - s

            @pl.when(jnp.logical_and(k >= 0, k < half))
            def _(s=s, k=k):
                stage(s, k)

        return carry

    lax.fori_loop(0, half + stages - 1, wave, 0)

    for step in range(1, n_az):
        give_pieces(step).wait_send()
    swap_g().wait_send()

    def finish(k, carry):
        swap_in(k).wait_send()
        for level in range(LEVELS):
            z_a(level, k).wait_send()
            z_i(level, k).wait_send()

            @pl.when(has_below)
            def _():
                ax_a(level, k).wait_send()

            @pl.when(has_above)
            def _():
                ax_i(level, k).wait_send()

        for which in range(2):
            out_here(which, k).wait()
            out_away(which, k).wait()
        return carry

    lax.fori_loop(0, half, finish, 0)


def shards(n_az, n_ax, start_field, reluctivity, lamination, magnets, region_ids, pieces, slot_map):
    devs, comps, cells, rows, radial = start_field.shape
    slots = pieces.shape[2]
    half, planes = devs // 2, 2 * cells
    lanes = -(-comps * devs // 128) * 128
    depth = -(-slots // 8) * 8
    wide = jnp.pad(
        jnp.transpose(pieces, (2, 0, 1)).reshape(slots, comps * devs),
        ((0, depth - slots), (0, lanes - comps * devs)),
    )
    base = lax.axis_index("az") // 2 * (2 * slots)
    own = lax.dynamic_slice_in_dim(slot_map, base, 2 * slots, 1).T
    own = jnp.pad(jnp.tile(own, (1, comps)), ((0, 0), (0, lanes - comps * devs)))

    tile = (rows, radial)
    dma = pltpu.SemaphoreType.DMA
    phase = (LEVELS, half)
    vmem, anywhere = pl.BlockSpec(memory_space=pltpu.VMEM), pl.BlockSpec(memory_space=pl.ANY)
    block = (half, comps, planes) + tile
    shape = jax.ShapeDtypeStruct(start_field.shape, F32)
    return pl.pallas_call(
        functools.partial(kernel, n_az, n_ax, devs, cells, slots),
        out_shape=(shape, shape),
        in_specs=[anywhere] + [vmem] * 6,
        out_specs=(anywhere, anywhere),
        scratch_shapes=[
            pltpu.VMEM((LEVELS,) + block, F32),
            pltpu.VMEM(block, F32),
            pltpu.VMEM((LEVELS,) + block, F32),
            pltpu.VMEM(block, F32),
            pltpu.VMEM(block, F32),
            pltpu.VMEM((comps + 1, planes) + tile, F32),
            pltpu.VMEM((n_az, depth, lanes), F32),
            pltpu.VMEM((2 * slots, lanes), F32),
            pltpu.VMEM(phase + (2,) + tile, F32),
            pltpu.VMEM(phase + (2,) + tile, F32),
        ]
        + [pltpu.VMEM(phase + (2 * planes, radial), F32)] * 4
        + [dma, dma((half,)), dma((half,)), dma, dma, dma((n_az,)), dma((n_az,))]
        + [dma(phase)] * 8
        + [dma((2, half))] * 3,
        compiler_params=pltpu.CompilerParams(
            collective_id=0, has_side_effects=True, vmem_limit_bytes=40 * 1024 * 1024
        ),
        cost_estimate=pl.CostEstimate(
            flops=150 * start_field.size, bytes_accessed=12 * start_field.size, transcendentals=0
        ),
    )(start_field, reluctivity, lamination, magnets, region_ids, wide, own)


def solution(mesh):
    placed = (
        P(None, None, "az", "ax", None),
        P(None, "az", "ax", None),
        P("az", "ax", None),
        P("az", "ax", None),
        P("az", "ax", None),
        P(None, None, "az"),
        P(),
    )
    return jax.shard_map(
        functools.partial(shards, mesh.shape["az"], mesh.shape["ax"]),
        mesh=mesh,
        in_specs=placed,
        out_specs=(P(None, None, "az", "ax", None), P(None, None, "az", "ax", None)),
        check_vma=False,
    )
```

time: 155 us -> 82.8 us (0.53)
  Pallas kernels: 0 us -> 73.1 us
  waiting for transfers between devices: 66.1 us -> 0 us
  blocking collectives: 35.3 us -> 0 us
  starting transfers between devices: 23.6 us -> 0 us
  other arithmetic: 16.3 us -> 0 us
  local copies, waits for them, and re-layouts: 12.4 us -> 8.56 us
    pallas_call x0 -> x1, Pallas kernels: none -> 73.1 us  [shards(): pl.pallas_call(functools.partial(kernel, n_az, n_ax, devs, cells, slots),...]
    ppermute x12 -> x0, waiting for transfers between devices: 66.1 us -> none  [the longest x6 65.3 us: passed_along(): return lax.ppermute(value, axis, pairs)]
    all_gather x1 -> x0, blocking collectives: 35.3 us -> none  [shards(): every_piece = lax.all_gather(pieces, 'az', axis=2, tiled=True)]
    ppermute x12 -> x0, starting transfers between devices: 23.6 us -> none  [the longest x6 13.2 us: passed_along(): return lax.ppermute(value, axis, pairs)]
    sub x19 -> x0, other arithmetic: 7.69 us -> none  [the longest x1 2.79 us: residual_shifts(): return -curl - mass_term * field]
    slice x19 -> x0, local copies, waits for them, and re-layouts: 7.02 us -> none  [the longest x3 2.44 us: residual_shifts(): field[:, 1:3, 1:]]
    unnamed x17 -> x14, local copies, waits for them, and re-layouts: 0.75 us -> 7.54 us
    another operation x18 -> x0, other arithmetic: 3.73 us -> none  [the longest x3 1.19 us: curl_backward(): jnp.stack([along_z2 - radial_backward(core[:, 1]), radial_backward(core[:...]
  transfers between devices with their start and end apart: 12 -> 0, of which waited for: 8 -> 0; matrix products, arithmetic and copies ran while one was open for 8% -> 0% of each run, Pallas kernels for 0% -> 0%
where the time goes in v1:
time: 82.8 us; the launch traced here: 82.4 us
  Pallas kernels  73.1 us (88%)
  local copies, waits for them, and re-layouts  8.56 us (10%)
    pallas_call x1, Pallas kernels, shards(): pl.pallas_call(functools.partial(kernel, n_az, n_ax, devs, cells, slots),...  73.1 us
    unnamed x14, local copies, waits for them, and re-layouts  7.54 us

profile of v1, /device:TPU:0, one launch (start us, length us, event | category | flops | bytes accessed | tf_op | source)
XLA Modules:
  0.0 82.4 jit_solution(6741291651885485901)
XLA Ops:
  0.6 0.0 copy-start
  0.7 0.7 copy-done
  1.3 0.1 dynamic-slice_bitcast_fusion
  1.4 0.1 copy.12
  1.5 0.7 copy.11
  2.2 0.1 reshape.11
  2.3 0.1 tile.10
  2.4 0.0 copy-start.1
  2.4 1.4 %copy-done.1 = f32[16,3,2,8,512]{4,3,2,1,0:T(8,128)S(1)} copy-done((f32[16,3,2,8,512]{4,3,2,1,0:T(8,128)S(1)}, f32[16,3,2,8,512]{4,3,2,1,0:T(8,128)}, u32[]{:S(2)}) %copy-start.1) | copy-done | bytes 1572888
  3.8 0.0 copy-start.2
  3.8 0.9 %copy-done.2 = f32[3,2,8,512]{3,2,1,0:T(8,128)S(1)} copy-done((f32[3,2,8,512]{3,2,1,0:T(8,128)S(1)}, f32[3,2,8,512]{3,2,1,0:T(8,128)}, u32[]{:S(2)}) %copy-start.2) | copy-done | bytes 98328
  4.7 0.0 copy-start.3
  4.7 0.8 copy-done.3
  5.4 0.0 copy-start.4
  5.4 0.8 copy-done.4
  6.2 0.0 copy-start.5
  6.2 0.8 copy-done.5
  6.9 73.1 %shard_map.86 = (f32[16,3,2,8,512]{4,3,2,1,0:T(8,128)S(1)}, f32[16,3,2,8,512]{4,3,2,1,0:T(8,128)S(1)}) custom-call(f32[16,3,2,8,512]{4,3,2,1,0:T(8,128)S(1)} %copy-done.1, f32[3,2,8,512]{3,2,1,0:T(8,128)S(1)} %copy-done.2, s32[2,8,512]{2,1,0:T(8,128)S(1)} %copy-done.3, s32[2,8,512]{2,1,0:T(8,128)S(1)} %copy-done.4, s32[2,8,512]{2,1,0:T(8,128)S(1)} %copy-done.5, ...), custom_call_target="tpu_custom_call" | custom-call | flops 58982400 | bytes 4718592 | tf_op jit(solution)/shard_map/pallas_call | solution.py:326
  80.1 1.1 %copy.15 = f32[16,3,2,8,512]{4,3,2,1,0:T(8,128)} copy(f32[16,3,2,8,512]{4,3,2,1,0:T(8,128)S(1)} %get-tuple-element.4) | data formatting | bytes 3145728
  81.2 1.1 %copy.16 = f32[16,3,2,8,512]{4,3,2,1,0:T(8,128)} copy(f32[16,3,2,8,512]{4,3,2,1,0:T(8,128)S(1)} %get-tuple-element.5) | data formatting | bytes 3145728
  (3 shorter events, 0.0 us)
Async XLA Ops:
  0.6 0.7 copy-start
  2.4 1.4 %copy-start.1 = (f32[16,3,2,8,512]{4,3,2,1,0:T(8,128)S(1)}, f32[16,3,2,8,512]{4,3,2,1,0:T(8,128)}, u32[]{:S(2)}) copy-start(f32[16,3,2,8,512]{4,3,2,1,0:T(8,128)} %start.1) | copy-start | bytes 4718596
  3.8 0.9 %copy-start.2 = (f32[3,2,8,512]{3,2,1,0:T(8,128)S(1)}, f32[3,2,8,512]{3,2,1,0:T(8,128)}, u32[]{:S(2)}) copy-start(f32[3,2,8,512]{3,2,1,0:T(8,128)} %rel.1) | copy-start | bytes 294916
  4.7 0.8 copy-start.3
  5.4 0.8 copy-start.4
  6.2 0.8 copy-start.5

commit v2 on v1

--- a/solution.py
+++ b/solution.py
@@ -21,10 +21,11 @@
 
 def kernel(
     n_az, n_ax, devs, cells, slots,
-    start, rel, lam, mag, reg, pcs, smap,
+    start, rel_in, lam_in, mag_in, reg_in, pcs_in, smap_in,
     sol, res,
+    rel, lam, mag, reg, pcs, smap,
     X, D0, I, NS, RS, G, PG, TAB, ZA, ZI, AA, AI, SA, SI,
-    in_loc, in_s, in_r, g_s, g_r, p_s, p_r,
+    ops, in_loc, in_s, in_r, g_s, g_r, p_s, p_r,
     za_s, za_r, zi_s, zi_r, aa_s, aa_r, ai_s, ai_r, o_s, o_r, o_l,
 ):
     half = devs // 2
@@ -83,6 +84,14 @@
         src, dst = ((X.at[2, k], sol), (RS.at[k], res))[which]
         return pltpu.make_async_copy(src.at[:, mine], dst.at[half * side + k], o_l.at[which, k])
 
+    operands = [
+        pltpu.make_async_copy(src, dst, ops.at[j])
+        for j, (src, dst) in enumerate(
+            ((rel_in, rel), (lam_in, lam), (mag_in, mag), (reg_in, reg), (pcs_in, pcs), (smap_in, smap))
+        )
+    ]
+    for copy in operands:
+        copy.start()
     local_in().start()
     barrier = pltpu.get_barrier_semaphore()
     for step in range(1, n_az):
@@ -98,6 +107,8 @@
     def _():
         pl.semaphore_signal(barrier, inc=1, device_id={"ax": ax + 1}, device_id_type=MESH)
 
+    for copy in operands:
+        copy.wait()
     for p in range(cells):
         G[0, cells * side + p] = rel[0, p]
         G[1, cells * side + p] = rel[1, p] * (1.0 + 3.0 * lam[p].astype(F32))
@@ -153,11 +164,9 @@
 
     def sources(k):
         table = TAB[...]
-        lane = lax.broadcasted_iota(jnp.int32, table.shape, 1)
+        lane = lax.broadcasted_iota(jnp.int32, table.shape[1:], 1)
         for c in range(3):
-            column = jnp.sum(
-                jnp.where(lane == c * devs + half * side + k, table, 0.0), axis=1, keepdims=True
-            )
+            column = jnp.sum(jnp.where(lane == half * side + k, table[c], 0.0), axis=1, keepdims=True)
             values = [jnp.broadcast_to(column[j : j + 1], (rows, radial)) for j in range(2 * slots)]
             for p in range(planes):
                 code = G[3, p]
@@ -248,12 +257,13 @@
                     give_pieces(step).wait_recv()
                 own = smap[...]
 
-                def add(p, total):
-                    for q in range(slots):
-                        total = total + jnp.where(own == p * slots + q, PG[p, q : q + 1, :], 0.0)
-                    return total
-
-                TAB[...] = lax.fori_loop(0, n_az, add, jnp.zeros(TAB.shape, F32))
+                for c in range(3):
+                    def add(p, total, c=c):
+                        for q in range(slots):
+                            total = total + jnp.where(own == p * slots + q, PG[p, c, q : q + 1, :], 0.0)
+                        return total
+
+                    TAB[c] = lax.fori_loop(0, n_az, add, jnp.zeros(own.shape, F32))
                 swap_g().wait_recv()
 
             sources(k)
@@ -307,50 +317,50 @@
     devs, comps, cells, rows, radial = start_field.shape
     slots = pieces.shape[2]
     half, planes = devs // 2, 2 * cells
-    lanes = -(-comps * devs // 128) * 128
-    depth = -(-slots // 8) * 8
-    wide = jnp.pad(
-        jnp.transpose(pieces, (2, 0, 1)).reshape(slots, comps * devs),
-        ((0, depth - slots), (0, lanes - comps * devs)),
-    )
+    by_slot = jnp.transpose(pieces, (0, 2, 1))
     base = lax.axis_index("az") // 2 * (2 * slots)
     own = lax.dynamic_slice_in_dim(slot_map, base, 2 * slots, 1).T
-    own = jnp.pad(jnp.tile(own, (1, comps)), ((0, 0), (0, lanes - comps * devs)))
 
     tile = (rows, radial)
     dma = pltpu.SemaphoreType.DMA
     phase = (LEVELS, half)
-    vmem, anywhere = pl.BlockSpec(memory_space=pltpu.VMEM), pl.BlockSpec(memory_space=pl.ANY)
+    anywhere = pl.BlockSpec(memory_space=pl.ANY)
     block = (half, comps, planes) + tile
     shape = jax.ShapeDtypeStruct(start_field.shape, F32)
     return pl.pallas_call(
         functools.partial(kernel, n_az, n_ax, devs, cells, slots),
         out_shape=(shape, shape),
-        in_specs=[anywhere] + [vmem] * 6,
+        in_specs=[anywhere] * 7,
         out_specs=(anywhere, anywhere),
         scratch_shapes=[
+            pltpu.VMEM(reluctivity.shape, F32),
+            pltpu.VMEM(lamination.shape, jnp.int32),
+            pltpu.VMEM(lamination.shape, jnp.int32),
+            pltpu.VMEM(lamination.shape, jnp.int32),
+            pltpu.VMEM(by_slot.shape, F32),
+            pltpu.VMEM(own.shape, jnp.int32),
             pltpu.VMEM((LEVELS,) + block, F32),
             pltpu.VMEM(block, F32),
             pltpu.VMEM((LEVELS,) + block, F32),
             pltpu.VMEM(block, F32),
             pltpu.VMEM(block, F32),
             pltpu.VMEM((comps + 1, planes) + tile, F32),
-            pltpu.VMEM((n_az, depth, lanes), F32),
-            pltpu.VMEM((2 * slots, lanes), F32),
+            pltpu.VMEM((n_az,) + by_slot.shape, F32),
+            pltpu.VMEM((comps,) + own.shape, F32),
             pltpu.VMEM(phase + (2,) + tile, F32),
             pltpu.VMEM(phase + (2,) + tile, F32),
         ]
         + [pltpu.VMEM(phase + (2 * planes, radial), F32)] * 4
-        + [dma, dma((half,)), dma((half,)), dma, dma, dma((n_az,)), dma((n_az,))]
+        + [dma((6,)), dma, dma((half,)), dma((half,)), dma, dma, dma((n_az,)), dma((n_az,))]
         + [dma(phase)] * 8
         + [dma((2, half))] * 3,
         compiler_params=pltpu.CompilerParams(
-            collective_id=0, has_side_effects=True, vmem_limit_bytes=40 * 1024 * 1024
+            collective_id=0, has_side_effects=True, vmem_limit_bytes=60 * 1024 * 1024
         ),
         cost_estimate=pl.CostEstimate(
             flops=150 * start_field.size, bytes_accessed=12 * start_field.size, transcendentals=0
         ),
-    )(start_field, reluctivity, lamination, magnets, region_ids, wide, own)
+    )(start_field, reluctivity, lamination, magnets, region_ids, by_slot, own)
 
 
 def solution(mesh):

time: 82.8 us -> 79.7 us (0.963)
  local copies, waits for them, and re-layouts: 8.56 us -> 5.44 us
    unnamed x14 -> x7, local copies, waits for them, and re-layouts: 7.54 us -> 5.37 us
    transpose x3 -> x0, local copies, waits for them, and re-layouts: 0.84 us -> none  [the longest x1 0.7 us: shards(): jnp.transpose(pieces, (2, 0, 1)).reshape(slots, comps * devs)]
where the time goes in v2:
time: 79.7 us; the launch traced here: 79.5 us
  Pallas kernels  73.4 us (92%)
  local copies, waits for them, and re-layouts  5.44 us (7%)
    pallas_call x1, Pallas kernels, shards(): pl.pallas_call(functools.partial(kernel, n_az, n_ax, devs, cells, slots),...  73.4 us
    unnamed x7, local copies, waits for them, and re-layouts  5.37 us

profile of v2, /device:TPU:0, one launch (start us, length us, event | category | flops | bytes accessed | tf_op | source)
XLA Modules:
  0.0 79.5 jit_solution(6035860770442274602)
XLA Ops:
  0.6 0.0 copy-start
  0.7 0.7 copy-done
  1.3 0.1 constant_dynamic-slice_fusion
  1.4 0.7 copy.10
  2.1 73.4 %shard_map.86 = (f32[16,3,2,8,512]{4,3,2,1,0:T(8,128)}, f32[16,3,2,8,512]{4,3,2,1,0:T(8,128)}) custom-call(f32[16,3,2,8,512]{4,3,2,1,0:T(8,128)} %start.1, f32[3,2,8,512]{3,2,1,0:T(8,128)} %rel_in.1, s32[2,8,512]{2,1,0:T(8,128)} %lam_in.1, s32[2,8,512]{2,1,0:T(8,128)} %mag_in.1, s32[2,8,512]{2,1,0:T(8,128)} %reg_in.1, f32[3,4,16]{2,1,0:T(4,128)} %bitcast.3, ...), custom_call_target="tpu_custom_call" | custom-call | flops 58982400 | bytes 4718592 | tf_op jit(solution)/shard_map/pallas_call | solution.py:330
  75.5 0.0 copy-start.1
  75.5 2.9 %copy.13 = f32[16,3,2,8,512]{4,3,2,1,0:T(8,128)} copy(f32[16,3,2,8,512]{4,3,2,1,0:T(8,128)} %get-tuple-element.4) | data formatting | bytes 3145728
  78.4 0.0 copy-done.1
  78.4 1.1 %copy.14 = f32[16,3,2,8,512]{4,3,2,1,0:T(8,128)} copy(f32[16,3,2,8,512]{4,3,2,1,0:T(8,128)S(1)} %copy-done.1) | data formatting | bytes 3145728
Async XLA Ops:
  0.6 0.7 copy-start
  75.5 2.9 %copy-start.1 = (f32[16,3,2,8,512]{4,3,2,1,0:T(8,128)S(1)}, f32[16,3,2,8,512]{4,3,2,1,0:T(8,128)}, u32[]{:S(2)}) copy-start(f32[16,3,2,8,512]{4,3,2,1,0:T(8,128)} %get-tuple-element.5) | copy-start | bytes 4718596

commit v3 on v2

--- a/solution.py
+++ b/solution.py
@@ -25,8 +25,10 @@
     sol, res,
     rel, lam, mag, reg, pcs, smap,
     X, D0, I, NS, RS, G, PG, TAB, ZA, ZI, AA, AI, SA, SI,
+    XF, IF, RF, HA, HI, FA, FI, SFA, SFI,
     ops, in_loc, in_s, in_r, g_s, g_r, p_s, p_r,
-    za_s, za_r, zi_s, zi_r, aa_s, aa_r, ai_s, ai_r, o_s, o_r, o_l,
+    za_s, za_r, zi_s, zi_r, aa_s, aa_r, ai_s, ai_r, o_l, f_l,
+    xf_s, xf_r, ha_s, ha_r, hi_s, hi_r, fa_s, fa_r, fi_s, fi_r,
 ):
     half = devs // 2
     planes = 2 * cells
@@ -74,15 +76,28 @@
     def ax_i(level, k):
         return remote(SI.at[level, k], AI.at[level, k], ai_s.at[level, k], ai_r.at[level, k], {"ax": ax + 1})
 
-    def out_away(which, k):
-        src, dst = ((X.at[2, k], sol), (RS.at[k], res))[which]
-        return remote(
-            src.at[:, theirs], dst.at[half * side + k], o_s.at[which, k], o_r.at[which, k], {"az": partner}
-        )
-
     def out_here(which, k):
-        src, dst = ((X.at[2, k], sol), (RS.at[k], res))[which]
-        return pltpu.make_async_copy(src.at[:, mine], dst.at[half * side + k], o_l.at[which, k])
+        src, dst = ((X.at[2, k, :, mine], sol), (RS.at[k], res))[which]
+        return pltpu.make_async_copy(src, dst.at[half * side + k], o_l.at[which, k])
+
+    def out_foreign(which, k):
+        src, dst = ((XF.at[k], sol), (RF.at[k], res))[which]
+        return pltpu.make_async_copy(src, dst.at[half * (1 - side) + k], f_l.at[which, k])
+
+    def hand_x(k):
+        return remote(X.at[2, k, :, theirs], XF.at[k], xf_s.at[k], xf_r.at[k], {"az": partner})
+
+    def hand_a(k, src):
+        return remote(src, HA.at[k], ha_s.at[k], ha_r.at[k], {"az": partner})
+
+    def hand_i(k, src):
+        return remote(src, HI.at[k], hi_s.at[k], hi_r.at[k], {"az": partner})
+
+    def far_a(k):
+        return remote(SFA.at[k], FA.at[k], fa_s.at[k], fa_r.at[k], {"ax": ax - 1})
+
+    def far_i(k):
+        return remote(SFI.at[k], FI.at[k], fi_s.at[k], fi_r.at[k], {"ax": ax + 1})
 
     operands = [
         pltpu.make_async_copy(src, dst, ops.at[j])
@@ -132,10 +147,12 @@
     @pl.when(jnp.logical_not(has_above))
     def _():
         AA[...] = jnp.zeros_like(AA)
+        FA[...] = jnp.zeros_like(FA)
 
     @pl.when(jnp.logical_not(has_below))
     def _():
         AI[...] = jnp.zeros_like(AI)
+        FI[...] = jnp.zeros_like(FI)
 
     row_of = lax.broadcasted_iota(jnp.int32, (rows, radial), 0)
     lane_of = lax.broadcasted_iota(jnp.int32, (rows, radial), 1)
@@ -151,6 +168,20 @@
 
     def prev_axial(v, halo):
         return jnp.where(row_of == 0, halo, pltpu.roll(v, 1, 0))
+
+    def flux_of(a0, a1, a2, b1, b2, h0, h2):
+        return (
+            (next_axial(a2, h2) - a2) - (next_radial(a1) - a1),
+            (next_radial(a0) - a0) - (b2 - a2),
+            (b1 - a1) - (next_axial(a0, h0) - a0),
+        )
+
+    def curl_of(i0, i1, i2, b1, b2, h0, h2):
+        return (
+            (i2 - prev_axial(i2, h2)) - (i1 - prev_radial(i1)),
+            (i0 - prev_radial(i0)) - (i2 - b2),
+            (i1 - b1) - (i0 - prev_axial(i0, h0)),
+        )
 
     def send_a(level, k):
         z_a(level, k).start()
@@ -190,10 +221,8 @@
                 b1, b2 = ZA[level, k, 0], ZA[level, k, 1]
             h0 = AA[level, k, p : p + 1, :]
             h2 = AA[level, k, planes + p : planes + p + 1, :]
-            f0 = (next_axial(a2, h2) - a2) - (next_radial(a1) - a1)
-            f1 = (next_radial(a0) - a0) - (b2 - a2)
-            f2 = (b1 - a1) - (next_axial(a0, h0) - a0)
-            for c, f in enumerate((f0, f1, f2)):
+            flux = flux_of(a0, a1, a2, b1, b2, h0, h2)
+            for c, f in enumerate(flux):
                 value = G[c, p] * f - NS[k, c, p]
                 I[level, k, c, p] = value
                 if c != 1:
@@ -221,26 +250,123 @@
                 b1, b2 = ZI[level, k, 0], ZI[level, k, 1]
             h0 = AI[level, k, p : p + 1, :]
             h2 = AI[level, k, planes + p : planes + p + 1, :]
-            c0 = (i2 - prev_axial(i2, h2)) - (i1 - prev_radial(i1))
-            c1 = (i0 - prev_radial(i0)) - (i2 - b2)
-            c2 = (i1 - b1) - (i0 - prev_axial(i0, h0))
-            for c, value in enumerate((c0, c1, c2)):
+            turned = curl_of(i0, i1, i2, b1, b2, h0, h2)
+            for c, value in enumerate(turned):
                 field = X[level, k, c, p]
                 r = -value - mass_term * field
                 if level == 0:
                     d = r * (1.0 / cheb_centre)
                     D0[k, c, p] = d
                     X[1, k, c, p] = field + d
-                elif level == 1:
+                else:
                     d = (rho_second * rho_first) * D0[k, c, p] + (2.0 * rho_second / cheb_halfwidth) * r
                     X[2, k, c, p] = field + d
-                else:
-                    RS[k, c, p] = r
-        if level < 2:
-            send_a(level + 1, k)
-        if level > 0:
-            out_away(level - 1, k).start()
-            out_here(level - 1, k).start()
+        send_a(level + 1, k)
+        if level == 1:
+            hand_x(k).start()
+            out_here(0, k).start()
+
+    def hand_ahead(k):
+        @pl.when(side == 0)
+        def _():
+            hand_a(k, ZA.at[2, k]).start()
+            hand_i(k, I.at[2, k, 1:3, cells - 1]).start()
+
+        @pl.when(side == 1)
+        def _():
+            hand_a(k, X.at[2, k, 1:3, cells]).start()
+
+    def last_curl(k):
+        z_i(2, k).wait_recv()
+
+        @pl.when(side == 1)
+        def _():
+            hand_i(k, ZI.at[2, k]).start()
+
+        @pl.when(has_below)
+        def _():
+            ax_i(2, k).wait_recv()
+
+        for q in range(cells):
+            p = cells * side + q
+            i0, i1, i2 = I[2, k, 0, p], I[2, k, 1, p], I[2, k, 2, p]
+            if q > 0:
+                b1, b2 = I[2, k, 1, p - 1], I[2, k, 2, p - 1]
+            else:
+                b1 = jnp.where(side == 0, ZI[2, k, 0], I[2, k, 1, cells - 1])
+                b2 = jnp.where(side == 0, ZI[2, k, 1], I[2, k, 2, cells - 1])
+            h0, h2 = (
+                jnp.where(side == 0, AI[2, k, at : at + 1, :], AI[2, k, at + cells : at + cells + 1, :])
+                for at in (q, planes + q)
+            )
+            for c, value in enumerate(curl_of(i0, i1, i2, b1, b2, h0, h2)):
+                RS[k, c, q] = -value - mass_term * X[2, k, c, p]
+        out_here(1, k).start()
+
+    def far_start(k):
+        hand_x(k).wait_recv()
+        out_foreign(0, k).start()
+        for q in range(cells):
+            for j, c in enumerate((0, 2)):
+                SFA[k, j * cells + q : j * cells + q + 1, :] = XF[k, c, q, 0:1, :]
+
+        @pl.when(has_below)
+        def _():
+            far_a(k).start()
+
+    def far_intensity(k):
+        hand_a(k, ZA.at[2, k]).wait_recv()
+
+        @pl.when(has_above)
+        def _():
+            far_a(k).wait_recv()
+
+        table = TAB[...]
+        lane = lax.broadcasted_iota(jnp.int32, table.shape[1:], 1)
+        for q in range(cells):
+            p = cells * side + q
+            a0, a1, a2 = XF[k, 0, q], XF[k, 1, q], XF[k, 2, q]
+            if q < cells - 1:
+                b1, b2 = XF[k, 1, q + 1], XF[k, 2, q + 1]
+            else:
+                b1, b2 = HA[k, 0], HA[k, 1]
+            h0, h2 = FA[k, q : q + 1, :], FA[k, cells + q : cells + q + 1, :]
+            code = G[3, p]
+            for c, f in enumerate(flux_of(a0, a1, a2, b1, b2, h0, h2)):
+                column = jnp.sum(
+                    jnp.where(lane == half * (1 - side) + k, table[c], 0.0), axis=1, keepdims=True
+                )
+                total = jnp.zeros((rows, radial), F32)
+                for j in range(slots):
+                    own = jnp.where(side == 0, column[j : j + 1], column[slots + j : slots + j + 1])
+                    total = jnp.where(code == float(j), jnp.broadcast_to(own, (rows, radial)), total)
+                value = G[c, p] * (f - total)
+                IF[k, c, q] = value
+                if c != 1:
+                    at = (0 if c == 0 else cells) + q
+                    SFI[k, at : at + 1, :] = value[rows - 1 : rows, :]
+
+        @pl.when(has_above)
+        def _():
+            far_i(k).start()
+
+    def far_curl(k):
+        hand_i(k, ZI.at[2, k]).wait_recv()
+
+        @pl.when(has_below)
+        def _():
+            far_i(k).wait_recv()
+
+        for q in range(cells):
+            i0, i1, i2 = IF[k, 0, q], IF[k, 1, q], IF[k, 2, q]
+            if q > 0:
+                b1, b2 = IF[k, 1, q - 1], IF[k, 2, q - 1]
+            else:
+                b1, b2 = HI[k, 0], HI[k, 1]
+            h0, h2 = FI[k, q : q + 1, :], FI[k, cells + q : cells + q + 1, :]
+            for c, value in enumerate(curl_of(i0, i1, i2, b1, b2, h0, h2)):
+                RF[k, c, q] = -value - mass_term * XF[k, c, q]
+        out_foreign(1, k).start()
 
     def stage(s, k):
         if s == 0:
@@ -268,12 +394,22 @@
 
             sources(k)
             intensity(0, k)
+        elif s == 5:
+            intensity(2, k)
+            hand_ahead(k)
+        elif s == 6:
+            last_curl(k)
+            far_start(k)
+        elif s == 7:
+            far_intensity(k)
+        elif s == 8:
+            far_curl(k)
         elif s % 2 == 0:
             curl(s // 2 - 1, k)
         else:
             intensity(s // 2, k)
 
-    stages = 1 + 2 * LEVELS
+    stages = 3 + 2 * LEVELS
 
     def wave(t, carry):
         for s in reversed(range(stages)):
@@ -305,9 +441,21 @@
             def _():
                 ax_i(level, k).wait_send()
 
+        hand_x(k).wait_send()
+        hand_a(k, ZA.at[2, k]).wait_send()
+        hand_i(k, ZI.at[2, k]).wait_send()
+
+        @pl.when(has_below)
+        def _():
+            far_a(k).wait_send()
+
+        @pl.when(has_above)
+        def _():
+            far_i(k).wait_send()
+
         for which in range(2):
             out_here(which, k).wait()
-            out_away(which, k).wait()
+            out_foreign(which, k).wait()
         return carry
 
     lax.fori_loop(0, half, finish, 0)
@@ -326,6 +474,7 @@
     phase = (LEVELS, half)
     anywhere = pl.BlockSpec(memory_space=pl.ANY)
     block = (half, comps, planes) + tile
+    home = (half, comps, cells) + tile
     shape = jax.ShapeDtypeStruct(start_field.shape, F32)
     return pl.pallas_call(
         functools.partial(kernel, n_az, n_ax, devs, cells, slots),
@@ -343,7 +492,7 @@
             pltpu.VMEM(block, F32),
             pltpu.VMEM((LEVELS,) + block, F32),
             pltpu.VMEM(block, F32),
-            pltpu.VMEM(block, F32),
+            pltpu.VMEM(home, F32),
             pltpu.VMEM((comps + 1, planes) + tile, F32),
             pltpu.VMEM((n_az,) + by_slot.shape, F32),
             pltpu.VMEM((comps,) + own.shape, F32),
@@ -351,9 +500,13 @@
             pltpu.VMEM(phase + (2,) + tile, F32),
         ]
         + [pltpu.VMEM(phase + (2 * planes, radial), F32)] * 4
+        + [pltpu.VMEM(home, F32)] * 3
+        + [pltpu.VMEM((half, 2) + tile, F32)] * 2
+        + [pltpu.VMEM((half, 2 * cells, radial), F32)] * 4
         + [dma((6,)), dma, dma((half,)), dma((half,)), dma, dma, dma((n_az,)), dma((n_az,))]
         + [dma(phase)] * 8
-        + [dma((2, half))] * 3,
+        + [dma((2, half))] * 2
+        + [dma((half,))] * 10,
         compiler_params=pltpu.CompilerParams(
             collective_id=0, has_side_effects=True, vmem_limit_bytes=60 * 1024 * 1024
         ),

time: 79.7 us -> 80.8 us (1.014)
  no operation moved by 1% of the time
where the time goes in v3:
time: 80.8 us; the launch traced here: 79.8 us
  Pallas kernels  73.7 us (91%)
  local copies, waits for them, and re-layouts  5.44 us (7%)
    pallas_call x1, Pallas kernels, shards(): pl.pallas_call(functools.partial(kernel, n_az, n_ax, devs, cells, slots),...  73.7 us
    unnamed x7, local copies, waits for them, and re-layouts  5.37 us

profile of v3, /device:TPU:0, one launch (start us, length us, event | category | flops | bytes accessed | tf_op | source)
XLA Modules:
  0.0 79.8 jit_solution(15904334369134415149)
XLA Ops:
  0.6 0.0 copy-start
  0.7 0.7 copy-done
  1.3 0.1 constant_dynamic-slice_fusion
  1.4 0.7 copy.10
  2.1 73.7 %shard_map.86 = (f32[16,3,2,8,512]{4,3,2,1,0:T(8,128)}, f32[16,3,2,8,512]{4,3,2,1,0:T(8,128)}) custom-call(f32[16,3,2,8,512]{4,3,2,1,0:T(8,128)} %start.1, f32[3,2,8,512]{3,2,1,0:T(8,128)} %rel_in.1, s32[2,8,512]{2,1,0:T(8,128)} %lam_in.1, s32[2,8,512]{2,1,0:T(8,128)} %mag_in.1, s32[2,8,512]{2,1,0:T(8,128)} %reg_in.1, f32[3,4,16]{2,1,0:T(4,128)} %bitcast.3, ...), custom_call_target="tpu_custom_call" | custom-call | flops 58982400 | bytes 4718592 | tf_op jit(solution)/shard_map/pallas_call | solution.py:479
  75.8 0.0 copy-start.1
  75.8 2.9 %copy.13 = f32[16,3,2,8,512]{4,3,2,1,0:T(8,128)} copy(f32[16,3,2,8,512]{4,3,2,1,0:T(8,128)} %get-tuple-element.4) | data formatting | bytes 3145728
  78.7 0.0 copy-done.1
  78.7 1.1 %copy.14 = f32[16,3,2,8,512]{4,3,2,1,0:T(8,128)} copy(f32[16,3,2,8,512]{4,3,2,1,0:T(8,128)S(1)} %copy-done.1) | data formatting | bytes 3145728
Async XLA Ops:
  0.6 0.7 copy-start
  75.8 2.9 %copy-start.1 = (f32[16,3,2,8,512]{4,3,2,1,0:T(8,128)S(1)}, f32[16,3,2,8,512]{4,3,2,1,0:T(8,128)}, u32[]{:S(2)}) copy-start(f32[16,3,2,8,512]{4,3,2,1,0:T(8,128)} %get-tuple-element.5) | copy-start | bytes 4718596

commit v4 on v2

--- a/solution.py
+++ b/solution.py
@@ -17,6 +17,7 @@
 MESH = pl.DeviceIdType.MESH
 F32 = jnp.float32
 LEVELS = 3
+GROUP = 2
 
 
 def kernel(
@@ -277,15 +278,19 @@
 
     def wave(t, carry):
         for s in reversed(range(stages)):
-            k = t - s
-
-            @pl.when(jnp.logical_and(k >= 0, k < half))
-            def _(s=s, k=k):
-                stage(s, k)
+            chunk = t - s
+
+            @pl.when(jnp.logical_and(chunk >= 0, chunk < half // GROUP))
+            def _(s=s, chunk=chunk):
+                def one(d, inner):
+                    stage(s, chunk * GROUP + d)
+                    return inner
+
+                lax.fori_loop(0, GROUP, one, 0)
 
         return carry
 
-    lax.fori_loop(0, half + stages - 1, wave, 0)
+    lax.fori_loop(0, half // GROUP + stages - 1, wave, 0)
 
     for step in range(1, n_az):
         give_pieces(step).wait_send()

time: 79.7 us -> 77.8 us (0.976)
  Pallas kernels: 73.4 us -> 71.5 us
    pallas_call x1, Pallas kernels: 73.4 us -> 71.5 us  [shards(): pl.pallas_call(functools.partial(kernel, n_az, n_ax, devs, cells, slots),...]
where the time goes in v4:
time: 77.8 us; the launch traced here: 77.6 us
  Pallas kernels  71.5 us (92%)
  local copies, waits for them, and re-layouts  5.44 us (7%)
    pallas_call x1, Pallas kernels, shards(): pl.pallas_call(functools.partial(kernel, n_az, n_ax, devs, cells, slots),...  71.5 us
    unnamed x7, local copies, waits for them, and re-layouts  5.37 us

profile of v4, /device:TPU:0, one launch (start us, length us, event | category | flops | bytes accessed | tf_op | source)
XLA Modules:
  0.0 77.6 jit_solution(16061319624863703440)
XLA Ops:
  0.6 0.0 copy-start
  0.7 0.7 copy-done
  1.3 0.1 constant_dynamic-slice_fusion
  1.4 0.7 copy.10
  2.1 71.5 %shard_map.86 = (f32[16,3,2,8,512]{4,3,2,1,0:T(8,128)}, f32[16,3,2,8,512]{4,3,2,1,0:T(8,128)}) custom-call(f32[16,3,2,8,512]{4,3,2,1,0:T(8,128)} %start.1, f32[3,2,8,512]{3,2,1,0:T(8,128)} %rel_in.1, s32[2,8,512]{2,1,0:T(8,128)} %lam_in.1, s32[2,8,512]{2,1,0:T(8,128)} %mag_in.1, s32[2,8,512]{2,1,0:T(8,128)} %reg_in.1, f32[3,4,16]{2,1,0:T(4,128)} %bitcast.3, ...), custom_call_target="tpu_custom_call" | custom-call | flops 58982400 | bytes 4718592 | tf_op jit(solution)/shard_map/pallas_call | solution.py:335
  73.6 0.0 copy-start.1
  73.6 2.9 %copy.13 = f32[16,3,2,8,512]{4,3,2,1,0:T(8,128)} copy(f32[16,3,2,8,512]{4,3,2,1,0:T(8,128)} %get-tuple-element.4) | data formatting | bytes 3145728
  76.5 0.0 copy-done.1
  76.5 1.1 %copy.14 = f32[16,3,2,8,512]{4,3,2,1,0:T(8,128)} copy(f32[16,3,2,8,512]{4,3,2,1,0:T(8,128)S(1)} %copy-done.1) | data formatting | bytes 3145728
Async XLA Ops:
  0.6 0.7 copy-start
  73.6 2.9 %copy-start.1 = (f32[16,3,2,8,512]{4,3,2,1,0:T(8,128)S(1)}, f32[16,3,2,8,512]{4,3,2,1,0:T(8,128)}, u32[]{:S(2)}) copy-start(f32[16,3,2,8,512]{4,3,2,1,0:T(8,128)} %get-tuple-element.5) | copy-start | bytes 4718596

commit v5 on v4

--- a/solution.py
+++ b/solution.py
@@ -18,6 +18,7 @@
 F32 = jnp.float32
 LEVELS = 3
 GROUP = 2
+AHEAD = 2
 
 
 def kernel(
@@ -124,11 +125,8 @@
         give_pieces(step).start()
     swap_g().start()
 
-    def start_in(k, carry):
+    for k in range(1, AHEAD):
         swap_in(k).start()
-        return carry
-
-    lax.fori_loop(1, half, start_in, 0)
 
     @pl.when(jnp.logical_not(has_above))
     def _():
@@ -250,6 +248,11 @@
                 local_in().wait()
 
             swap_in(k).wait_recv()
+
+            @pl.when(k + AHEAD < half)
+            def _():
+                swap_in(k + AHEAD).start()
+
             send_a(0, k)
         elif s == 1:
             @pl.when(k == 0)

time: 77.8 us -> 77.5 us (level)
  no operation moved by 1% of the time
where the time goes in v5:
time: 77.5 us; the launch traced here: 77.3 us
  Pallas kernels  71.2 us (92%)
  local copies, waits for them, and re-layouts  5.44 us (7%)
    pallas_call x1, Pallas kernels, shards(): pl.pallas_call(functools.partial(kernel, n_az, n_ax, devs, cells, slots),...  71.2 us
    unnamed x7, local copies, waits for them, and re-layouts  5.37 us

profile of v5, /device:TPU:0, one launch (start us, length us, event | category | flops | bytes accessed | tf_op | source)
XLA Modules:
  0.0 77.3 jit_solution(17661591914672733013)
XLA Ops:
  0.6 0.0 copy-start
  0.7 0.7 copy-done
  1.3 0.1 constant_dynamic-slice_fusion
  1.4 0.7 copy.10
  2.1 71.2 %shard_map.86 = (f32[16,3,2,8,512]{4,3,2,1,0:T(8,128)}, f32[16,3,2,8,512]{4,3,2,1,0:T(8,128)}) custom-call(f32[16,3,2,8,512]{4,3,2,1,0:T(8,128)} %start.1, f32[3,2,8,512]{3,2,1,0:T(8,128)} %rel_in.1, s32[2,8,512]{2,1,0:T(8,128)} %lam_in.1, s32[2,8,512]{2,1,0:T(8,128)} %mag_in.1, s32[2,8,512]{2,1,0:T(8,128)} %reg_in.1, f32[3,4,16]{2,1,0:T(4,128)} %bitcast.3, ...), custom_call_target="tpu_custom_call" | custom-call | flops 58982400 | bytes 4718592 | tf_op jit(solution)/shard_map/pallas_call | solution.py:338
  73.2 0.0 copy-start.1
  73.2 2.9 %copy.13 = f32[16,3,2,8,512]{4,3,2,1,0:T(8,128)} copy(f32[16,3,2,8,512]{4,3,2,1,0:T(8,128)} %get-tuple-element.4) | data formatting | bytes 3145728
  76.1 0.0 copy-done.1
  76.1 1.1 %copy.14 = f32[16,3,2,8,512]{4,3,2,1,0:T(8,128)} copy(f32[16,3,2,8,512]{4,3,2,1,0:T(8,128)S(1)} %copy-done.1) | data formatting | bytes 3145728
Async XLA Ops:
  0.6 0.7 copy-start
  73.2 2.9 %copy-start.1 = (f32[16,3,2,8,512]{4,3,2,1,0:T(8,128)S(1)}, f32[16,3,2,8,512]{4,3,2,1,0:T(8,128)}, u32[]{:S(2)}) copy-start(f32[16,3,2,8,512]{4,3,2,1,0:T(8,128)} %get-tuple-element.5) | copy-start | bytes 4718596

commit v6 on v3

--- a/solution.py
+++ b/solution.py
@@ -17,6 +17,9 @@
 MESH = pl.DeviceIdType.MESH
 F32 = jnp.float32
 LEVELS = 3
+GROUP = 2
+AHEAD = 3
+PLAIN = 2
 
 
 def kernel(
@@ -27,10 +30,11 @@
     X, D0, I, NS, RS, G, PG, TAB, ZA, ZI, AA, AI, SA, SI,
     XF, IF, RF, HA, HI, FA, FI, SFA, SFI,
     ops, in_loc, in_s, in_r, g_s, g_r, p_s, p_r,
-    za_s, za_r, zi_s, zi_r, aa_s, aa_r, ai_s, ai_r, o_l, f_l,
+    za_s, za_r, zi_s, zi_r, aa_s, aa_r, ai_s, ai_r, o_l, f_l, o_s, o_r,
     xf_s, xf_r, ha_s, ha_r, hi_s, hi_r, fa_s, fa_r, fi_s, fi_r,
 ):
     half = devs // 2
+    short = half - PLAIN
     planes = 2 * cells
     rows, radial = X.shape[-2], X.shape[-1]
     az, ax = lax.axis_index("az"), lax.axis_index("ax")
@@ -77,8 +81,14 @@
         return remote(SI.at[level, k], AI.at[level, k], ai_s.at[level, k], ai_r.at[level, k], {"ax": ax + 1})
 
     def out_here(which, k):
-        src, dst = ((X.at[2, k, :, mine], sol), (RS.at[k], res))[which]
-        return pltpu.make_async_copy(src, dst.at[half * side + k], o_l.at[which, k])
+        src, dst = ((X.at[2, k], sol), (RS.at[k], res))[which]
+        return pltpu.make_async_copy(src.at[:, mine], dst.at[half * side + k], o_l.at[which, k])
+
+    def out_away(which, k):
+        src, dst = ((X.at[2, k], sol), (RS.at[k], res))[which]
+        return remote(
+            src.at[:, theirs], dst.at[half * side + k], o_s.at[which, k], o_r.at[which, k], {"az": partner}
+        )
 
     def out_foreign(which, k):
         src, dst = ((XF.at[k], sol), (RF.at[k], res))[which]
@@ -138,11 +148,8 @@
         give_pieces(step).start()
     swap_g().start()
 
-    def start_in(k, carry):
+    for k in range(1, AHEAD):
         swap_in(k).start()
-        return carry
-
-    lax.fori_loop(1, half, start_in, 0)
 
     @pl.when(jnp.logical_not(has_above))
     def _():
@@ -254,16 +261,29 @@
             for c, value in enumerate(turned):
                 field = X[level, k, c, p]
                 r = -value - mass_term * field
-                if level == 0:
+                if level == 2:
+                    RS[k, c, p] = r
+                elif level == 0:
                     d = r * (1.0 / cheb_centre)
                     D0[k, c, p] = d
                     X[1, k, c, p] = field + d
                 else:
                     d = (rho_second * rho_first) * D0[k, c, p] + (2.0 * rho_second / cheb_halfwidth) * r
                     X[2, k, c, p] = field + d
-        send_a(level + 1, k)
+        if level == 2:
+            out_away(1, k).start()
+            out_here(1, k).start()
+        else:
+            send_a(level + 1, k)
         if level == 1:
-            hand_x(k).start()
+            @pl.when(k < short)
+            def _():
+                hand_x(k).start()
+
+            @pl.when(k >= short)
+            def _():
+                out_away(0, k).start()
+
             out_here(0, k).start()
 
     def hand_ahead(k):
@@ -300,7 +320,7 @@
                 for at in (q, planes + q)
             )
             for c, value in enumerate(curl_of(i0, i1, i2, b1, b2, h0, h2)):
-                RS[k, c, q] = -value - mass_term * X[2, k, c, p]
+                RS[k, c, p] = -value - mass_term * X[2, k, c, p]
         out_here(1, k).start()
 
     def far_start(k):
@@ -375,6 +395,11 @@
                 local_in().wait()
 
             swap_in(k).wait_recv()
+
+            @pl.when(k + AHEAD < half)
+            def _():
+                swap_in(k + AHEAD).start()
+
             send_a(0, k)
         elif s == 1:
             @pl.when(k == 0)
@@ -396,32 +421,40 @@
             intensity(0, k)
         elif s == 5:
             intensity(2, k)
-            hand_ahead(k)
+
+            @pl.when(k < short)
+            def _():
+                hand_ahead(k)
         elif s == 6:
-            last_curl(k)
-            far_start(k)
-        elif s == 7:
-            far_intensity(k)
-        elif s == 8:
-            far_curl(k)
+            @pl.when(k < short)
+            def _():
+                last_curl(k)
+
+            @pl.when(k >= short)
+            def _():
+                curl(2, k)
         elif s % 2 == 0:
             curl(s // 2 - 1, k)
         else:
             intensity(s // 2, k)
 
-    stages = 3 + 2 * LEVELS
+    def grouped(work, chunk, count):
+        @pl.when(jnp.logical_and(chunk >= 0, chunk < count // GROUP))
+        def _():
+            def one(d, inner):
+                work(chunk * GROUP + d)
+                return inner
+
+            lax.fori_loop(0, GROUP, one, 0)
 
     def wave(t, carry):
-        for s in reversed(range(stages)):
-            k = t - s
-
-            @pl.when(jnp.logical_and(k >= 0, k < half))
-            def _(s=s, k=k):
-                stage(s, k)
-
+        for s in reversed(range(1 + 2 * LEVELS)):
+            grouped(functools.partial(stage, s), t - s, half)
+        for s, work in ((8, far_curl), (7, far_intensity), (6, far_start)):
+            grouped(work, t - s, short)
         return carry
 
-    lax.fori_loop(0, half + stages - 1, wave, 0)
+    lax.fori_loop(0, max(half // GROUP + 6, short // GROUP + 8), wave, 0)
 
     for step in range(1, n_az):
         give_pieces(step).wait_send()
@@ -441,6 +474,13 @@
             def _():
                 ax_i(level, k).wait_send()
 
+        for which in range(2):
+            out_here(which, k).wait()
+        return carry
+
+    lax.fori_loop(0, half, finish, 0)
+
+    def finish_short(k, carry):
         hand_x(k).wait_send()
         hand_a(k, ZA.at[2, k]).wait_send()
         hand_i(k, ZI.at[2, k]).wait_send()
@@ -454,11 +494,30 @@
             far_i(k).wait_send()
 
         for which in range(2):
-            out_here(which, k).wait()
             out_foreign(which, k).wait()
         return carry
 
-    lax.fori_loop(0, half, finish, 0)
+    lax.fori_loop(0, short, finish_short, 0)
+
+    def finish_plain(k, carry):
+        for which in range(2):
+            out_away(which, k).wait()
+        return carry
+
+    lax.fori_loop(short, half, finish_plain, 0)
+
+
+def hand_over(a, b, a_out, b_out, sems):
+    pieces = a.shape[0] // 4
+    copies = [
+        pltpu.make_async_copy(src.at[pl.ds(j * pieces, pieces)], dst.at[pl.ds(j * pieces, pieces)], sems.at[i, j])
+        for i, (src, dst) in enumerate(((a, a_out), (b, b_out)))
+        for j in range(4)
+    ]
+    for copy in copies:
+        copy.start()
+    for copy in copies:
+        copy.wait()
 
 
 def shards(n_az, n_ax, start_field, reluctivity, lamination, magnets, region_ids, pieces, slot_map):
@@ -476,7 +535,7 @@
     block = (half, comps, planes) + tile
     home = (half, comps, cells) + tile
     shape = jax.ShapeDtypeStruct(start_field.shape, F32)
-    return pl.pallas_call(
+    field, left = pl.pallas_call(
         functools.partial(kernel, n_az, n_ax, devs, cells, slots),
         out_shape=(shape, shape),
         in_specs=[anywhere] * 7,
@@ -492,7 +551,7 @@
             pltpu.VMEM(block, F32),
             pltpu.VMEM((LEVELS,) + block, F32),
             pltpu.VMEM(block, F32),
-            pltpu.VMEM(home, F32),
+            pltpu.VMEM(block, F32),
             pltpu.VMEM((comps + 1, planes) + tile, F32),
             pltpu.VMEM((n_az,) + by_slot.shape, F32),
             pltpu.VMEM((comps,) + own.shape, F32),
@@ -505,7 +564,7 @@
         + [pltpu.VMEM((half, 2 * cells, radial), F32)] * 4
         + [dma((6,)), dma, dma((half,)), dma((half,)), dma, dma, dma((n_az,)), dma((n_az,))]
         + [dma(phase)] * 8
-        + [dma((2, half))] * 2
+        + [dma((2, half))] * 4
         + [dma((half,))] * 10,
         compiler_params=pltpu.CompilerParams(
             collective_id=0, has_side_effects=True, vmem_limit_bytes=60 * 1024 * 1024
@@ -514,6 +573,15 @@
             flops=150 * start_field.size, bytes_accessed=12 * start_field.size, transcendentals=0
         ),
     )(start_field, reluctivity, lamination, magnets, region_ids, by_slot, own)
+    return pl.pallas_call(
+        hand_over,
+        out_shape=(shape, shape),
+        in_specs=[anywhere] * 2,
+        out_specs=(anywhere, anywhere),
+        scratch_shapes=[dma((2, 4))],
+        compiler_params=pltpu.CompilerParams(vmem_limit_bytes=60 * 1024 * 1024),
+        cost_estimate=pl.CostEstimate(flops=0, bytes_accessed=16 * start_field.size, transcendentals=0),
+    )(field, left)
 
 
 def solution(mesh):

time: 80.8 us -> 166 us (2.05)
  Pallas kernels: 73.7 us -> 164 us
  local copies, waits for them, and re-layouts: 5.44 us -> 1.41 us
    pallas_call x0 -> x1, Pallas kernels: none -> 96.5 us  [shards(): pl.pallas_call(hand_over, out_shape=(shape, shape), in_specs=[anywhere] *...]
    pallas_call x1, Pallas kernels: 73.7 us -> 67.2 us  [shards(): pl.pallas_call(functools.partial(kernel, n_az, n_ax, devs, cells, slots),...]
    unnamed x7 -> x3, local copies, waits for them, and re-layouts: 5.37 us -> 1.34 us
where the time goes in v6:
time: 166 us
  Pallas kernels  164 us (99%)
    pallas_call x1, Pallas kernels, shards(): pl.pallas_call(hand_over, out_shape=(shape, shape), in_specs=[anywhere] *...  96.5 us
    pallas_call x1, Pallas kernels, shards(): pl.pallas_call(functools.partial(kernel, n_az, n_ax, devs, cells, slots),...  67.2 us

profile of v6, /device:TPU:0, one launch (start us, length us, event | category | flops | bytes accessed | tf_op | source)
XLA Modules:
  0.0 165.7 jit_solution(3974123134011219749)
XLA Ops:
  0.6 0.0 copy-start
  0.7 0.7 copy-done
  1.3 0.1 constant_dynamic-slice_fusion
  1.4 0.7 copy.10
  2.1 67.2 %shard_map.86 = (f32[16,3,2,8,512]{4,3,2,1,0:T(8,128)}, f32[16,3,2,8,512]{4,3,2,1,0:T(8,128)}) custom-call(f32[16,3,2,8,512]{4,3,2,1,0:T(8,128)} %start.1, f32[3,2,8,512]{3,2,1,0:T(8,128)} %rel_in.1, s32[2,8,512]{2,1,0:T(8,128)} %lam_in.1, s32[2,8,512]{2,1,0:T(8,128)} %mag_in.1, s32[2,8,512]{2,1,0:T(8,128)} %reg_in.1, f32[3,4,16]{2,1,0:T(4,128)} %bitcast.3, ...), custom_call_target="tpu_custom_call" | custom-call | flops 58982400 | bytes 4718592 | tf_op jit(solution)/shard_map/pallas_call | solution.py:538
  69.3 96.5 %shard_map.87 = (f32[16,3,2,8,512]{4,3,2,1,0:T(8,128)}, f32[16,3,2,8,512]{4,3,2,1,0:T(8,128)}) custom-call(f32[16,3,2,8,512]{4,3,2,1,0:T(8,128)} %get-tuple-element.4.a, f32[16,3,2,8,512]{4,3,2,1,0:T(8,128)} %get-tuple-element.5.b), custom_call_target="tpu_custom_call" | custom-call | bytes 6291456 | tf_op jit(solution)/shard_map/pallas_call | solution.py:576
Async XLA Ops:
  0.6 0.7 copy-start

commit v7 on v6

--- a/solution.py
+++ b/solution.py
@@ -26,7 +26,7 @@
     n_az, n_ax, devs, cells, slots,
     start, rel_in, lam_in, mag_in, reg_in, pcs_in, smap_in,
     sol, res,
-    rel, lam, mag, reg, pcs, smap,
+    rel, lam, mag, reg, pcs, smap, turned_map,
     X, D0, I, NS, RS, G, PG, TAB, ZA, ZI, AA, AI, SA, SI,
     XF, IF, RF, HA, HI, FA, FI, SFA, SFI,
     ops, in_loc, in_s, in_r, g_s, g_r, p_s, p_r,
@@ -406,12 +406,16 @@
             def _():
                 for step in range(1, n_az):
                     give_pieces(step).wait_recv()
-                own = smap[...]
+                turned_map[...] = jnp.zeros_like(turned_map)
+                turned_map[0:devs, 0 : smap.shape[1]] = smap[...].astype(F32)
+                turned_map[...] = jnp.transpose(turned_map[...])
+                base = pl.multiple_of((az - side) * slots, 2 * slots)
+                own = turned_map[pl.ds(base, 2 * slots), 0:devs]
 
                 for c in range(3):
                     def add(p, total, c=c):
                         for q in range(slots):
-                            total = total + jnp.where(own == p * slots + q, PG[p, c, q : q + 1, :], 0.0)
+                            total = total + jnp.where(own == (p * slots + q).astype(F32), PG[p, c, q : q + 1, :], 0.0)
                         return total
 
                     TAB[c] = lax.fori_loop(0, n_az, add, jnp.zeros(own.shape, F32))
@@ -507,17 +511,26 @@
     lax.fori_loop(short, half, finish_plain, 0)
 
 
-def hand_over(a, b, a_out, b_out, sems):
-    pieces = a.shape[0] // 4
-    copies = [
-        pltpu.make_async_copy(src.at[pl.ds(j * pieces, pieces)], dst.at[pl.ds(j * pieces, pieces)], sems.at[i, j])
-        for i, (src, dst) in enumerate(((a, a_out), (b, b_out)))
-        for j in range(4)
-    ]
-    for copy in copies:
-        copy.start()
-    for copy in copies:
-        copy.wait()
+def hand_over(a, b, a_out, b_out, held, in_sems, out_sems):
+    parts = in_sems.shape[1]
+    share = a.shape[0] // parts
+
+    def pair(i, j):
+        src, dst = ((a, a_out), (b, b_out))[i]
+        rows = pl.ds(j * share, share)
+        return (
+            pltpu.make_async_copy(src.at[rows], held.at[i, rows], in_sems.at[i, j]),
+            pltpu.make_async_copy(held.at[i, rows], dst.at[rows], out_sems.at[i, j]),
+        )
+
+    pairs = [pair(i, j) for j in range(parts) for i in range(2)]
+    for first, _ in pairs:
+        first.start()
+    for first, second in pairs:
+        first.wait()
+        second.start()
+    for _, second in pairs:
+        second.wait()
 
 
 def shards(n_az, n_ax, start_field, reluctivity, lamination, magnets, region_ids, pieces, slot_map):
@@ -525,8 +538,8 @@
     slots = pieces.shape[2]
     half, planes = devs // 2, 2 * cells
     by_slot = jnp.transpose(pieces, (0, 2, 1))
-    base = lax.axis_index("az") // 2 * (2 * slots)
-    own = lax.dynamic_slice_in_dim(slot_map, base, 2 * slots, 1).T
+    regions = slot_map.shape[1]
+    square = -(-max(regions, devs) // 128) * 128
 
     tile = (rows, radial)
     dma = pltpu.SemaphoreType.DMA
@@ -546,7 +559,8 @@
             pltpu.VMEM(lamination.shape, jnp.int32),
             pltpu.VMEM(lamination.shape, jnp.int32),
             pltpu.VMEM(by_slot.shape, F32),
-            pltpu.VMEM(own.shape, jnp.int32),
+            pltpu.VMEM(slot_map.shape, jnp.int32),
+            pltpu.VMEM((square, square), F32),
             pltpu.VMEM((LEVELS,) + block, F32),
             pltpu.VMEM(block, F32),
             pltpu.VMEM((LEVELS,) + block, F32),
@@ -554,7 +568,7 @@
             pltpu.VMEM(block, F32),
             pltpu.VMEM((comps + 1, planes) + tile, F32),
             pltpu.VMEM((n_az,) + by_slot.shape, F32),
-            pltpu.VMEM((comps,) + own.shape, F32),
+            pltpu.VMEM((comps, 2 * slots, devs), F32),
             pltpu.VMEM(phase + (2,) + tile, F32),
             pltpu.VMEM(phase + (2,) + tile, F32),
         ]
@@ -572,13 +586,13 @@
         cost_estimate=pl.CostEstimate(
             flops=150 * start_field.size, bytes_accessed=12 * start_field.size, transcendentals=0
         ),
-    )(start_field, reluctivity, lamination, magnets, region_ids, by_slot, own)
+    )(start_field, reluctivity, lamination, magnets, region_ids, by_slot, slot_map)
     return pl.pallas_call(
         hand_over,
         out_shape=(shape, shape),
         in_specs=[anywhere] * 2,
         out_specs=(anywhere, anywhere),
-        scratch_shapes=[dma((2, 4))],
+        scratch_shapes=[pltpu.VMEM((2,) + start_field.shape, F32), dma((2, 4)), dma((2, 4))],
         compiler_params=pltpu.CompilerParams(vmem_limit_bytes=60 * 1024 * 1024),
         cost_estimate=pl.CostEstimate(flops=0, bytes_accessed=16 * start_field.size, transcendentals=0),
     )(field, left)

time: 166 us -> 70.8 us (0.43)
  Pallas kernels: 164 us -> 70 us
    pallas_call x1, Pallas kernels: 96.5 us -> 2.79 us  [shards(): pl.pallas_call(hand_over, out_shape=(shape, shape), in_specs=[anywhere] *...]
where the time goes in v7:
time: 70.8 us; the launch traced here: 70.6 us
  Pallas kernels  70 us (99%)
    pallas_call x1, Pallas kernels, shards(): pl.pallas_call(functools.partial(kernel, n_az, n_ax, devs, cells, slots),...  67.2 us
    pallas_call x1, Pallas kernels, shards(): pl.pallas_call(hand_over, out_shape=(shape, shape), in_specs=[anywhere] *...  2.79 us

profile of v7, /device:TPU:0, one launch (start us, length us, event | category | flops | bytes accessed | tf_op | source)
XLA Modules:
  0.0 70.6 jit_solution(1925323284212504328)
XLA Ops:
  0.6 67.2 %shard_map.86 = (f32[16,3,2,8,512]{4,3,2,1,0:T(8,128)}, f32[16,3,2,8,512]{4,3,2,1,0:T(8,128)}) custom-call(f32[16,3,2,8,512]{4,3,2,1,0:T(8,128)} %start.1, f32[3,2,8,512]{3,2,1,0:T(8,128)} %rel_in.1, s32[2,8,512]{2,1,0:T(8,128)} %lam_in.1, s32[2,8,512]{2,1,0:T(8,128)} %mag_in.1, s32[2,8,512]{2,1,0:T(8,128)} %reg_in.1, f32[3,4,16]{2,1,0:T(4,128)} %bitcast.1, ...), custom_call_target="tpu_custom_call" | custom-call | flops 58982400 | bytes 4718592 | tf_op jit(solution)/shard_map/pallas_call | solution.py:551
  67.9 2.8 %shard_map.87 = (f32[16,3,2,8,512]{4,3,2,1,0:T(8,128)}, f32[16,3,2,8,512]{4,3,2,1,0:T(8,128)}) custom-call(f32[16,3,2,8,512]{4,3,2,1,0:T(8,128)} %get-tuple-element.4.a, f32[16,3,2,8,512]{4,3,2,1,0:T(8,128)} %get-tuple-element.5.b), custom_call_target="tpu_custom_call" | custom-call | bytes 6291456 | tf_op jit(solution)/shard_map/pallas_call | solution.py:590

commit v8 on v7

--- a/solution.py
+++ b/solution.py
@@ -17,7 +17,7 @@
 MESH = pl.DeviceIdType.MESH
 F32 = jnp.float32
 LEVELS = 3
-GROUP = 2
+GROUP = 1
 AHEAD = 3
 PLAIN = 2
 
@@ -454,11 +454,11 @@
     def wave(t, carry):
         for s in reversed(range(1 + 2 * LEVELS)):
             grouped(functools.partial(stage, s), t - s, half)
-        for s, work in ((8, far_curl), (7, far_intensity), (6, far_start)):
+        for s, work in ((9, far_curl), (8, far_intensity), (7, far_start)):
             grouped(work, t - s, short)
         return carry
 
-    lax.fori_loop(0, max(half // GROUP + 6, short // GROUP + 8), wave, 0)
+    lax.fori_loop(0, max(half // GROUP + 6, short // GROUP + 9), wave, 0)
 
     for step in range(1, n_az):
         give_pieces(step).wait_send()

time: 70.8 us -> 77.8 us (1.099)
  Pallas kernels: 70 us -> 77 us
    pallas_call x1, Pallas kernels: 67.2 us -> 74.3 us  [shards(): pl.pallas_call(functools.partial(kernel, n_az, n_ax, devs, cells, slots),...]
where the time goes in v8:
time: 77.8 us; the launch traced here: 77.7 us
  Pallas kernels  77 us (99%)
    pallas_call x1, Pallas kernels, shards(): pl.pallas_call(functools.partial(kernel, n_az, n_ax, devs, cells, slots),...  74.3 us
    pallas_call x1, Pallas kernels, shards(): pl.pallas_call(hand_over, out_shape=(shape, shape), in_specs=[anywhere] *...  2.79 us

profile of v8, /device:TPU:0, one launch (start us, length us, event | category | flops | bytes accessed | tf_op | source)
XLA Modules:
  0.0 77.7 jit_solution(11570560295377232084)
XLA Ops:
  0.6 74.3 %shard_map.86 = (f32[16,3,2,8,512]{4,3,2,1,0:T(8,128)}, f32[16,3,2,8,512]{4,3,2,1,0:T(8,128)}) custom-call(f32[16,3,2,8,512]{4,3,2,1,0:T(8,128)} %start.1, f32[3,2,8,512]{3,2,1,0:T(8,128)} %rel_in.1, s32[2,8,512]{2,1,0:T(8,128)} %lam_in.1, s32[2,8,512]{2,1,0:T(8,128)} %mag_in.1, s32[2,8,512]{2,1,0:T(8,128)} %reg_in.1, f32[3,4,16]{2,1,0:T(4,128)} %bitcast.1, ...), custom_call_target="tpu_custom_call" | custom-call | flops 58982400 | bytes 4718592 | tf_op jit(solution)/shard_map/pallas_call | solution.py:551
  74.9 2.8 %shard_map.87 = (f32[16,3,2,8,512]{4,3,2,1,0:T(8,128)}, f32[16,3,2,8,512]{4,3,2,1,0:T(8,128)}) custom-call(f32[16,3,2,8,512]{4,3,2,1,0:T(8,128)} %get-tuple-element.4.a, f32[16,3,2,8,512]{4,3,2,1,0:T(8,128)} %get-tuple-element.5.b), custom_call_target="tpu_custom_call" | custom-call | bytes 6291456 | tf_op jit(solution)/shard_map/pallas_call | solution.py:590

commit v9 on v7

--- a/solution.py
+++ b/solution.py
@@ -17,9 +17,9 @@
 MESH = pl.DeviceIdType.MESH
 F32 = jnp.float32
 LEVELS = 3
-GROUP = 2
-AHEAD = 3
-PLAIN = 2
+GROUP = 4
+AHEAD = 4
+PLAIN = 4
 
 
 def kernel(

time: 70.8 us -> 75.5 us (1.066)
  Pallas kernels: 70 us -> 74.7 us
    pallas_call x1, Pallas kernels: 67.2 us -> 71.9 us  [shards(): pl.pallas_call(functools.partial(kernel, n_az, n_ax, devs, cells, slots),...]
where the time goes in v9:
time: 75.5 us; the launch traced here: 75.4 us
  Pallas kernels  74.7 us (99%)
    pallas_call x1, Pallas kernels, shards(): pl.pallas_call(functools.partial(kernel, n_az, n_ax, devs, cells, slots),...  71.9 us
    pallas_call x1, Pallas kernels, shards(): pl.pallas_call(hand_over, out_shape=(shape, shape), in_specs=[anywhere] *...  2.79 us

profile of v9, /device:TPU:0, one launch (start us, length us, event | category | flops | bytes accessed | tf_op | source)
XLA Modules:
  0.0 75.4 jit_solution(11766278282961268918)
XLA Ops:
  0.6 71.9 %shard_map.86 = (f32[16,3,2,8,512]{4,3,2,1,0:T(8,128)}, f32[16,3,2,8,512]{4,3,2,1,0:T(8,128)}) custom-call(f32[16,3,2,8,512]{4,3,2,1,0:T(8,128)} %start.1, f32[3,2,8,512]{3,2,1,0:T(8,128)} %rel_in.1, s32[2,8,512]{2,1,0:T(8,128)} %lam_in.1, s32[2,8,512]{2,1,0:T(8,128)} %mag_in.1, s32[2,8,512]{2,1,0:T(8,128)} %reg_in.1, f32[3,4,16]{2,1,0:T(4,128)} %bitcast.1, ...), custom_call_target="tpu_custom_call" | custom-call | flops 58982400 | bytes 4718592 | tf_op jit(solution)/shard_map/pallas_call | solution.py:551
  72.6 2.8 %shard_map.87 = (f32[16,3,2,8,512]{4,3,2,1,0:T(8,128)}, f32[16,3,2,8,512]{4,3,2,1,0:T(8,128)}) custom-call(f32[16,3,2,8,512]{4,3,2,1,0:T(8,128)} %get-tuple-element.4.a, f32[16,3,2,8,512]{4,3,2,1,0:T(8,128)} %get-tuple-element.5.b), custom_call_target="tpu_custom_call" | custom-call | bytes 6291456 | tf_op jit(solution)/shard_map/pallas_call | solution.py:590

commit v10 on v7

--- a/solution.py
+++ b/solution.py
@@ -454,11 +454,11 @@
     def wave(t, carry):
         for s in reversed(range(1 + 2 * LEVELS)):
             grouped(functools.partial(stage, s), t - s, half)
-        for s, work in ((8, far_curl), (7, far_intensity), (6, far_start)):
+        for s, work in ((7, far_curl), (6, far_intensity), (5, far_start)):
             grouped(work, t - s, short)
         return carry
 
-    lax.fori_loop(0, max(half // GROUP + 6, short // GROUP + 8), wave, 0)
+    lax.fori_loop(0, max(half // GROUP + 6, short // GROUP + 7), wave, 0)
 
     for step in range(1, n_az):
         give_pieces(step).wait_send()

time: 70.8 us -> 70.8 us (level)
  no operation moved by 1% of the time
where the time goes in v10:
time: 70.8 us; the launch traced here: 70.6 us
  Pallas kernels  70 us (99%)
    pallas_call x1, Pallas kernels, shards(): pl.pallas_call(functools.partial(kernel, n_az, n_ax, devs, cells, slots),...  67.2 us
    pallas_call x1, Pallas kernels, shards(): pl.pallas_call(hand_over, out_shape=(shape, shape), in_specs=[anywhere] *...  2.79 us

profile of v10, /device:TPU:0, one launch (start us, length us, event | category | flops | bytes accessed | tf_op | source)
XLA Modules:
  0.0 70.6 jit_solution(5644426568458497475)
XLA Ops:
  0.6 67.2 %shard_map.86 = (f32[16,3,2,8,512]{4,3,2,1,0:T(8,128)}, f32[16,3,2,8,512]{4,3,2,1,0:T(8,128)}) custom-call(f32[16,3,2,8,512]{4,3,2,1,0:T(8,128)} %start.1, f32[3,2,8,512]{3,2,1,0:T(8,128)} %rel_in.1, s32[2,8,512]{2,1,0:T(8,128)} %lam_in.1, s32[2,8,512]{2,1,0:T(8,128)} %mag_in.1, s32[2,8,512]{2,1,0:T(8,128)} %reg_in.1, f32[3,4,16]{2,1,0:T(4,128)} %bitcast.1, ...), custom_call_target="tpu_custom_call" | custom-call | flops 58982400 | bytes 4718592 | tf_op jit(solution)/shard_map/pallas_call | solution.py:551
  67.9 2.8 %shard_map.87 = (f32[16,3,2,8,512]{4,3,2,1,0:T(8,128)}, f32[16,3,2,8,512]{4,3,2,1,0:T(8,128)}) custom-call(f32[16,3,2,8,512]{4,3,2,1,0:T(8,128)} %get-tuple-element.4.a, f32[16,3,2,8,512]{4,3,2,1,0:T(8,128)} %get-tuple-element.5.b), custom_call_target="tpu_custom_call" | custom-call | bytes 6291456 | tf_op jit(solution)/shard_map/pallas_call | solution.py:590
